TPU v7x, 256 devices: a whole 4x4x8 slice. The times are simulated.
256 devices in a mesh: dp: 8 (over z_lo, core), ctx: 32 (over x, z_hi, y).
Axes of the slice: x: 4, y: 4, z: 8 (z_hi: 2, z_lo: 4; z = z_hi * 4 + z_lo), core: 2. Of those that a mesh axis runs over, the one named last changes fastest.
Arguments:
- queries: bfloat16 [8, 4096, 12288], P('dp', 'ctx'), may hold values from -6 to 115
- grad_out: bfloat16 [8, 4096, 8192], P('dp', 'ctx'), may hold values from -6 to 6
- latent: bfloat16 [8, 4096, 576], P('dp', 'ctx'), may hold values from -6 to 6
- up_weight: bfloat16 [512, 16384], P(None, 'ctx'), may hold values from -0.25 to 0.25
- doc_lengths: int32 [8, 128], P('dp'), may hold values from 1 to 64, 4096 in all within a row
- stretch_order: int32 [8, 64], P('dp'), may hold values from 0 to 63, each once within a row
Outputs:
- grad_queries: bfloat16 [8, 4096, 12288], P('dp', 'ctx')
- grad_latent: bfloat16 [8, 4096, 576], P('dp', 'ctx')
- grad_weight: float32 [512, 16384], P(None, 'ctx')
Inputs may be any that keep to these rules, and one draw needn't show every extreme that they name: `doc_lengths`: each row sums to 4096 and its largest length is exactly 64. `stretch_order`: each row names every block once.
All inputs are finite; a program needn't handle non-finite values.
Results may differ from a plain program's by a relative error of at most 0.03.
Values may be sent and summed in bfloat16 or wider, within the bound.
A program may use at most 128 MiB of HBM per device.

v0:
```python
import jax
import jax.numpy as jnp
from jax import lax
from jax.sharding import PartitionSpec as P

D_NOPE = 128
D_ROPE = 64
D_V = 128
D_LAT = 512
QB = 512
DOC_MOST = 64


def pad_front(array, behind, filler):
    front_rows = jnp.full((behind,) + array.shape[1:], filler, array.dtype)
    return jnp.concatenate([front_rows, array], 0)


def fold_windows(windows, behind):
    front_part = windows[:, :behind]
    main_part = windows[:, behind:]
    carried = jnp.concatenate([front_part[1:], jnp.zeros_like(front_part[:1])], 0)
    main_part = main_part.at[:, QB - behind :].add(carried)
    return main_part.reshape((-1,) + main_part.shape[2:])


def banded(query_all, grad_all, keys_nope, values, keys_rope, doc_ids):
    tokens_all = query_all.shape[0]
    behind = DOC_MOST
    scale = (D_NOPE + D_ROPE) ** (-0.5)
    positions = jnp.arange(tokens_all, dtype=jnp.int32)
    keys_pad = pad_front(keys_nope, behind, 0)
    values_pad = pad_front(values, behind, 0)
    rotary_pad = pad_front(keys_rope, behind, 0)
    key_pos = pad_front(positions, behind, -1)
    key_doc = pad_front(doc_ids, behind, -1)
    f32 = jnp.float32

    def one_block(index):
        row_start = index * QB
        span = QB + behind
        query_blk = lax.dynamic_slice_in_dim(query_all, row_start, QB, 0)
        grad_blk = lax.dynamic_slice_in_dim(grad_all, row_start, QB, 0)
        key_blk = lax.dynamic_slice_in_dim(keys_pad, row_start, span, 0)
        value_blk = lax.dynamic_slice_in_dim(values_pad, row_start, span, 0)
        rotary_blk = lax.dynamic_slice_in_dim(rotary_pad, row_start, span, 0)
        pos_blk = lax.dynamic_slice_in_dim(key_pos, row_start, span, 0)
        doc_blk = lax.dynamic_slice_in_dim(key_doc, row_start, span, 0)
        query_pos = row_start + jnp.arange(QB, dtype=jnp.int32)
        query_doc = lax.dynamic_slice_in_dim(doc_ids, row_start, QB, 0)
        allowed = (pos_blk[None, :] <= query_pos[:, None]) & (
            doc_blk[None, :] == query_doc[:, None]
        )
        query_nope = query_blk[..., :D_NOPE]
        query_rope = query_blk[..., D_NOPE:]
        scores = (
            jnp.einsum("qhd,khd->hqk", query_nope, key_blk, preferred_element_type=f32)
            + jnp.einsum("qhd,kd->hqk", query_rope, rotary_blk, preferred_element_type=f32)
        ) * scale
        scores = jnp.where(allowed[None], scores, -jnp.inf)
        highest = jnp.max(scores, -1, keepdims=True)
        expo = jnp.exp(scores - highest)
        probs = expo / jnp.sum(expo, -1, keepdims=True)
        dprob = jnp.einsum("qhd,khd->hqk", grad_blk, value_blk, preferred_element_type=f32)
        delta = jnp.sum(probs * dprob, -1, keepdims=True)
        dscore = (probs * (dprob - delta) * scale).astype(jnp.bfloat16)
        probs_low = probs.astype(jnp.bfloat16)
        grad_nope = jnp.einsum("hqk,khd->qhd", dscore, key_blk, preferred_element_type=f32)
        grad_rope = jnp.einsum("hqk,kd->qhd", dscore, rotary_blk, preferred_element_type=f32)
        grad_query = jnp.concatenate([grad_nope, grad_rope], -1).astype(jnp.bfloat16)
        grad_values = jnp.einsum("hqk,qhd->khd", probs_low, grad_blk, preferred_element_type=f32)
        grad_keys = jnp.einsum("hqk,qhd->khd", dscore, query_nope, preferred_element_type=f32)
        grad_rotary = jnp.einsum("hqk,qhd->kd", dscore, query_rope, preferred_element_type=f32)
        return (grad_query, grad_keys, grad_values, grad_rotary)

    results = lax.map(one_block, jnp.arange(tokens_all // QB, dtype=jnp.int32))
    grad_query = results[0].reshape((tokens_all,) + results[0].shape[2:])
    return (
        grad_query,
        fold_windows(results[1], behind),
        fold_windows(results[2], behind),
        fold_windows(results[3], behind),
    )


def per_device(queries, grad_out, latent, up_weight, doc_lengths, stretch_order):
    count = lax.axis_size("ctx")
    query_heads, grad_heads = (
        lax.all_to_all(queries[0], "ctx", split_axis=1, concat_axis=0, tiled=True),
        lax.all_to_all(grad_out[0], "ctx", split_axis=1, concat_axis=0, tiled=True),
    )
    whole_latent = lax.all_gather(latent[0], "ctx", axis=0, tiled=True)
    tokens_all = whole_latent.shape[0]
    head_cols = D_NOPE + D_V
    local_heads = up_weight.shape[1] // head_cols
    stretch_rows = tokens_all // (2 * count)
    storage_order = stretch_order[0]
    inverse = jnp.argsort(storage_order)

    def to_natural(array):
        blocks = array.reshape((2 * count, stretch_rows) + array.shape[1:])
        return jnp.take(blocks, inverse, axis=0).reshape(array.shape)

    def to_storage(array):
        blocks = array.reshape((2 * count, stretch_rows) + array.shape[1:])
        return jnp.take(blocks, storage_order, axis=0).reshape(array.shape)

    ends = jnp.cumsum(doc_lengths[0])
    positions = jnp.arange(tokens_all, dtype=jnp.int32)
    doc_ids = jnp.sum((ends[None, :] <= positions[:, None]).astype(jnp.int32), 1)
    latent_nat = to_natural(whole_latent)
    query_nat = to_natural(query_heads).reshape(tokens_all, local_heads, D_NOPE + D_ROPE)
    grad_nat = to_natural(grad_heads).reshape(tokens_all, local_heads, D_V)
    keys_values = jnp.dot(
        latent_nat[:, :D_LAT], up_weight, preferred_element_type=jnp.float32
    ).astype(jnp.bfloat16)
    keys_values = keys_values.reshape(tokens_all, local_heads, head_cols)
    grad_query, grad_keys, grad_values, grad_rotary = banded(
        query_nat,
        grad_nat,
        keys_values[..., :D_NOPE],
        keys_values[..., D_NOPE:],
        latent_nat[:, D_LAT:],
        doc_ids,
    )
    grad_kv = (
        jnp.concatenate([grad_keys, grad_values], -1)
        .astype(jnp.bfloat16)
        .reshape(tokens_all, local_heads * head_cols)
    )
    weight_part = lax.dot_general(
        latent_nat[:, :D_LAT], grad_kv, (((0,), (0,)), ((), ())), preferred_element_type=jnp.float32
    )
    latent_part = lax.dot_general(
        grad_kv, up_weight, (((1,), (1,)), ((), ())), preferred_element_type=jnp.float32
    )
    partial_sums = to_storage(jnp.concatenate([latent_part, grad_rotary], 1).astype(jnp.bfloat16))
    query_back = to_storage(grad_query.reshape(tokens_all, local_heads * (D_NOPE + D_ROPE)))
    query_out = lax.all_to_all(query_back, "ctx", split_axis=0, concat_axis=1, tiled=True)
    latent_grad = lax.psum_scatter(
        partial_sums.astype(jnp.float32).astype(jnp.bfloat16),
        "ctx",
        scatter_dimension=0,
        tiled=True,
    )
    weight_grad = lax.psum(weight_part.astype(jnp.bfloat16), "dp").astype(jnp.float32)
    return (query_out[None], latent_grad[None], weight_grad)


def solution(mesh):
    in_specs = (
        P("dp", "ctx", None),
        P("dp", "ctx", None),
        P("dp", "ctx", None),
        P(None, "ctx"),
        P("dp", None),
        P("dp", None),
    )
    out_specs = (P("dp", "ctx", None), P("dp", "ctx", None), P(None, "ctx"))
    return jax.shard_map(
        per_device, mesh=mesh, in_specs=in_specs, out_specs=out_specs, check_vma=False
    )
```

profile of v0, /device:TPU:64, one launch (start us, length us, event | category | flops | bytes accessed | tf_op | source)
XLA Modules:
  0.0 995.4 jit_solution(4358973637290651461)
XLA Ops:
  11.3 12.3 %all-to-all-start.1 = ((bf16[128,32,256]{0,2,1:T(8,128)(2,1)}), bf16[128,32,256]{0,2,1:T(8,128)(2,1)S(1)}, u32[]{:S(2)}, u32[]{:S(2)}) async-start(bf16[128,32,256]{0,2,1:T(8,128)(2,1)} %bitcast.101), calls=%async_computation.1 | async-start | bytes 4194304 | tf_op jit(solution)/shard_map/all_to_all | solution.py:90
  29.1 50.8 %all-to-all-done.1 = bf16[128,32,256]{0,2,1:T(8,128)(2,1)S(1)} async-done(((bf16[128,32,256]{0,2,1:T(8,128)(2,1)}), bf16[128,32,256]{0,2,1:T(8,128)(2,1)S(1)}, u32[]{:S(2)}, u32[]{:S(2)}) %all-to-all-start.1) | async-done | bytes 2097184 | tf_op jit(solution)/shard_map/all_to_all | solution.py:90
  80.0 5.4 all-to-all-start
  99.2 15.2 %broadcast_select_fusion.2 = bf16[4096,2,128]{2,1,0:T(2,128)(2,1)} fusion(bf16[4096,2,128]{2,1,0:T(2,128)(2,1)S(1)} %gather.13, pred[4096]{0:T(1024)(128)(4,1)S(1)} %broadcast_in_dim.96), kind=kLoop, calls=%fused_computation.73 | loop fusion | flops 1048576 | bytes 4198400 | tf_op jit(solution)/shard_map/jit(_take)/select_n | solution.py:102
  114.4 48.5 %all-to-all-done = bf16[128,32,384]{0,2,1:T(8,128)(2,1)} async-done(((bf16[128,32,384]{0,2,1:T(8,128)(2,1)}), bf16[128,32,384]{0,2,1:T(8,128)(2,1)}, u32[]{:S(2)}, u32[]{:S(2)}) %all-to-all-start) | async-done | bytes 3145760 | tf_op jit(solution)/shard_map/all_to_all | solution.py:89
  176.2 10.2 %reshape_reshape.4 = bf16[4096,2,192]{2,1,0:T(2,128)(2,1)} reshape(bf16[64,64,384]{2,1,0:T(8,128)(2,1)} %broadcast_select_fusion.4) | data formatting | bytes 6291456 | tf_op jit(solution)/shard_map/reshape;reshape | solution.py:112
  189.4 6.0 gather_fusion.1
  217.2 301.3 %while.20 = (s32[]{:T(128)}, bf16[8,512,2,192]{1,3,2,0:T(8,128)(2,1)}, f32[8,576,2,128]{3,1,0,2:T(8,128)}, f32[8,576,2,128]{3,1,0,2:T(8,128)}, f32[8,576,64]{1,2...) while((s32[]{:T(128)}, ...), condition=%wide.region_7.10_spmd, body=%wide.region_3.9_spmd.sunk | while | flops 1004577664 | bytes 64652644 | solution.py:76
  230.6 5.5 fusion.144
  238.6 5.7 fusion.142
  244.4 5.0 fusion.141
  268.2 5.5 fusion.144
  276.1 5.8 fusion.142
  281.9 5.1 fusion.141
  305.8 5.5 fusion.144
  313.7 5.8 fusion.142
  319.5 5.1 fusion.141
  324.6 5.0 fusion.140
  343.4 5.5 fusion.144
  351.3 5.7 fusion.142
  357.1 5.0 fusion.141
  380.9 5.5 fusion.144
  389.0 5.7 fusion.142
  394.7 5.1 fusion.141
  418.6 5.5 fusion.144
  426.6 5.7 fusion.142
  432.3 5.1 fusion.141
  456.2 5.5 fusion.144
  464.1 5.7 fusion.142
  469.9 5.0 fusion.141
  493.7 5.5 fusion.144
  501.8 5.8 fusion.142
  507.5 5.1 fusion.141
  512.6 5.0 fusion.140
  527.5 27.4 %copy.108 = bf16[4096,2,256]{2,1,0:T(2,128)(2,1)} copy(bf16[4096,2,256]{2,0,1:T(8,128)(2,1)S(1)} %maximum_convert_fusion) | data formatting | bytes 8388608 | tf_op jit(solution)/shard_map/convert_element_type | solution.py:128
  554.8 6.4 copy.111
  561.2 7.6 convert_element_type.50
  568.9 6.6 convolution_convert_fusion.1
  577.7 6.6 fusion.80
  584.4 5.4 pad_maximum_fusion
  589.8 6.1 gather_fusion.4
  595.9 5.4 broadcast_select_fusion
  601.3 11.2 %copy.100 = bf16[8,512,2,192]{3,2,1,0:T(2,128)(2,1)} copy(bf16[8,512,2,192]{1,3,2,0:T(8,128)(2,1)} %get-tuple-element.157) | data formatting | bytes 6291456 | tf_op jit(solution)/shard_map/while | solution.py:76
  612.5 9.4 reshape_reshape_reshape.3
  630.7 23.5 %all-to-all-start.2 = ((bf16[32,128,384]{2,1,0:T(8,128)(2,1)}), bf16[32,128,384]{2,1,0:T(8,128)(2,1)}, u32[]{:S(2)}, u32[]{:S(2)}) async-start(bf16[32,128,384]{2,1,0:T(8,128)(2,1)} %bitcast.97), calls=%async_computation.2 | async-start | bytes 6291456 | tf_op jit(solution)/shard_map/all_to_all | solution.py:139
  654.2 24.0 %all-reduce.9.cloned.1.call-done = bf16[512,512]{1,0:T(8,128)(2,1)} async-done(((bf16[512,512]{1,0:T(8,128)(2,1)}), bf16[512,512]{1,0:T(8,128)(2,1)}) %all-reduce.9.cloned.1.call-update) | async-done | bytes 524304 | tf_op jit(solution)/shard_map/psum | solution.py:146
  680.3 38.9 %all-to-all-done.2 = bf16[32,128,384]{2,1,0:T(8,128)(2,1)} async-done(((bf16[32,128,384]{2,1,0:T(8,128)(2,1)}), bf16[32,128,384]{2,1,0:T(8,128)(2,1)}, u32[]{:S(2)}, u32[]{:S(2)}) %all-to-all-start.2) | async-done | bytes 3145760 | tf_op jit(solution)/shard_map/all_to_all | solution.py:139
  728.5 258.4 %reduce-scatter.4.cloned.1.call-done = bf16[128,576]{1,0:T(8,128)(2,1)} async-done(((bf16[4096,576]{1,0:T(8,128)(2,1)}), bf16[128,576]{1,0:T(8,128)(2,1)}) %reduce-scatter.4.cloned.1.call-update) | async-done | bytes 147472
  (219 shorter events, 249.2 us)
Async XLA Ops:
  7.2 192.5 %copy-start = (bf16[512,512]{1,0:T(8,128)(2,1)S(1)}, bf16[512,512]{1,0:T(8,128)(2,1)}, u32[]{:S(2)}) copy-start(bf16[512,512]{1,0:T(8,128)(2,1)} %param.21) | copy-start | bytes 1572868
  11.3 12.3 %copy-start.8 = (bf16[1,128,576]{1,2,0:T(8,128)(2,1)S(1)}, bf16[1,128,576]{1,2,0:T(8,128)(2,1)}, u32[]{:S(2)}) copy-start(bf16[1,128,576]{1,2,0:T(8,128)(2,1)} %param.20) | copy-start | bytes 442372
  11.3 68.6 %all-to-all-start.1 = ((bf16[128,32,256]{0,2,1:T(8,128)(2,1)}), bf16[128,32,256]{0,2,1:T(8,128)(2,1)S(1)}, u32[]{:S(2)}, u32[]{:S(2)}) async-start(bf16[128,32,256]{0,2,1:T(8,128)(2,1)} %bitcast.101), calls=%async_computation.1 | async-start | bytes 4194304 | tf_op jit(solution)/shard_map/all_to_all | solution.py:90
  23.6 165.8 %all-gather.3.cloned.1.call-start = ((), (), s32[]{:S(2)}) async-start(), calls=%async_computation.5 | async-start | bytes 5406720 | tf_op jit(solution)/shard_map/all_gather | solution.py:92
  79.9 5.5 copy-start.11
  79.9 7.8 copy-start.10
  80.0 83.0 %all-to-all-start = ((bf16[128,32,384]{0,2,1:T(8,128)(2,1)}), bf16[128,32,384]{0,2,1:T(8,128)(2,1)}, u32[]{:S(2)}, u32[]{:S(2)}) async-start(bf16[128,32,384]{0,2,1:T(8,128)(2,1)} %bitcast.96), calls=%async_computation | async-start | bytes 6291456 | tf_op jit(solution)/shard_map/all_to_all | solution.py:89
  85.4 592.8 %all-reduce.9.cloned.1.call-start = ((), (), s32[]{:S(2)}) async-start(), calls=%async_computation.4 | async-start | bytes 1048576 | tf_op jit(solution)/shard_map/psum | solution.py:146
  198.6 3.5 copy-start.4
  211.8 2.4 copy-start.3
  214.2 1.6 copy-start.5
  224.2 3.7 copy-start.2
  261.7 3.7 copy-start.2
  299.3 3.7 copy-start.2
  336.9 3.7 copy-start.2
  374.4 3.7 copy-start.2
  412.1 3.7 copy-start.2
  449.7 3.7 copy-start.2
  487.2 3.7 copy-start.2
  518.4 3.8 copy-start.6
  522.2 1.3 copy-start.7
  525.5 2.0 copy-start.1
  584.4 402.5 %reduce-scatter.4.cloned.1.call-start = ((), (), s32[]{:S(2)}) async-start(), calls=%async_computation.6 | async-start | bytes 5406720
  589.8 6.1 copy-start.9
  630.7 88.5 %all-to-all-start.2 = ((bf16[32,128,384]{2,1,0:T(8,128)(2,1)}), bf16[32,128,384]{2,1,0:T(8,128)(2,1)}, u32[]{:S(2)}, u32[]{:S(2)}) async-start(bf16[32,128,384]{2,1,0:T(8,128)(2,1)} %bitcast.97), calls=%async_computation.2 | async-start | bytes 6291456 | tf_op jit(solution)/shard_map/all_to_all | solution.py:139
Sparse Core Ops, SparseCore 0:
  28.4 160.9 all-gather.2
  584.5 93.6 all-reduce.8
  680.9 305.9 reduce-scatter.3
where the time goes:
time: 1010 us; the launch traced here: 995 us
  waiting for transfers between devices  424 us (42%)
  matrix products  254 us (25%)
  local copies, waits for them, and re-layouts  187 us (19%)
  other arithmetic  69.3 us (7%)
  starting transfers between devices  41.3 us (4%)
  between operations  14.3 us (1%)
    unnamed x4, waiting for transfers between devices  258 us
    all_to_all x1, waiting for transfers between devices, per_device(): lax.all_to_all(grad_out[0], 'ctx', split_axis=1, concat_axis=0, tiled=True)  50.8 us
    all_to_all x1, waiting for transfers between devices, per_device(): lax.all_to_all(queries[0], 'ctx', split_axis=1, concat_axis=0, tiled=True)  48.5 us
    dot_general x8, matrix products, one_block(): jnp.einsum('hqk,qhd->khd', dscore, query_nope, preferred_element_type=f32)  46 us
    dot_general x8, matrix products, one_block(): jnp.einsum('hqk,qhd->kd', dscore, query_rope, preferred_element_type=f32)  44.1 us
    convert_element_type x3, local copies, waits for them, and re-layouts, per_device(): grad_kv = jnp.concatenate([grad_keys, grad_values], -1).astype(jnp.bfloat...  41.4 us
    dot_general x8, matrix products, one_block(): jnp.einsum('hqk,khd->qhd', dscore, key_blk, preferred_element_type=f32)  40.5 us
    dot_general x8, matrix products, one_block(): jnp.einsum('hqk,kd->qhd', dscore, rotary_blk, preferred_element_type=f32)  39.8 us
  transfers between devices with their start and end apart: 6, of which 6 were waited for; matrix products, arithmetic and copies ran while one was open for 12% of the time, Pallas kernels for 0%

commit v1 on v0

v1 whole, which is shorter than its diff:
```python
import jax
import jax.numpy as jnp
from jax import lax
from jax.experimental import pallas as pl
from jax.experimental.pallas import tpu as pltpu
from jax.sharding import PartitionSpec as P


BF16 = jnp.bfloat16
F32 = jnp.float32
MESH = pl.DeviceIdType.MESH

D_NOPE = 128
D_ROPE = 64
D_V = 128
D_LAT = 512
D_ALL = D_LAT + D_ROPE
STRETCH = 64
OWN = 128
KEYS = 256
QW = 2 * (D_NOPE + D_ROPE)
VW = 2 * D_V
KVW = 2 * (D_NOPE + D_V)
SCALE = (D_NOPE + D_ROPE) ** -0.5
HALF = D_LAT // 2
QUARTER = D_LAT // 4
VMEM_LIMIT = 60 * 1024 * 1024


def gray(index):
    return index + index // 2 - 2 * (index // 3)


GRAY = [0, 1, 3, 2]
UNGRAY = [0, 1, 3, 2]


def slot_of(dx, dy):
    return 4 * UNGRAY[dy % 4] + UNGRAY[dx % 4]


def rows_of(half, piece):
    base = half * HALF
    if piece == "f":
        return base, HALF
    return base + int(piece) * QUARTER, QUARTER


def main_axis(half):
    return "x" if half == 0 else "y"


def at(axis, along, across):
    return (along, across) if axis == "x" else (across, along)


class Coords:
    def __init__(self):
        dp, ctx = lax.axis_index("dp"), lax.axis_index("ctx")
        self.dp, self.ctx = dp, ctx
        self.zl, self.core = dp // 2, dp % 2
        self.x, self.zh, self.y = ctx // 8, (ctx // 4) % 2, ctx % 4

    def device(self, x=None, y=None, zh=None, zl=None, core=None):
        x = self.x if x is None else x
        y = self.y if y is None else y
        zh = self.zh if zh is None else zh
        zl = self.zl if zl is None else zl
        core = self.core if core is None else core
        return (zl * 2 + core, (x * 2 + zh) * 4 + y)

    def neighbour(self, axis, sign):
        if axis == "x":
            return self.device(x=(self.x + 4 + sign) % 4)
        return self.device(y=(self.y + 4 + sign) % 4)


def gather_keys():
    keys = []
    for half in (0, 1):
        axis = main_axis(half)
        for across in range(4):
            for along in range(4):
                dx, dy = at(axis, along, across)
                if along == 0 and across == 0:
                    continue
                last = across if across else along
                for piece in ("0", "1") if last == 2 else ("f",):
                    keys.append((half, dx, dy, piece))
    return {key: i for i, key in enumerate(keys)}


GATHER = gather_keys()


def reduce_keys():
    keys, row = {}, 0
    for half in (0, 1):
        for across in range(4):
            for phase in (0, 1):
                if phase == 1 and across:
                    continue
                for piece, count in (("0", QUARTER), ("1", QUARTER), ("from1", HALF), ("from3", HALF)):
                    keys[(half, phase, across, piece)] = (len(keys), row, count)
                    row += count
    return keys, row


REDUCE, REDUCE_ROWS = reduce_keys()


def main_kernel(
    q_hbm,
    go_hbm,
    lat_ref,
    klo_ref,
    w_ref,
    gq_hbm,
    glat_ref,
    sum_ref,
    qbuf,
    gobuf,
    gqbuf,
    latb,
    lat_t,
    klob,
    bias,
    wbuf,
    gbuf,
    rbuf,
    kvbuf,
    gkvbuf,
    acc,
    accin,
    loc_q,
    loc_go,
    rem_q,
    rem_go,
    snd_q,
    snd_go,
    misc,
    wz,
    ag_send,
    ag_recv,
    rs_send,
    rs_recv,
    gq_loc,
    gq_snd,
    gq_rcv,
):
    me = Coords()
    core, other = me.core, 1 - me.core
    partner = me.device(core=other)
    is_source = me.zh == core
    up = me.zl >= 2
    sends_up = jnp.logical_and(is_source, me.zl == 3)
    sends_down = jnp.logical_and(is_source, me.zl == 0)
    z_source = me.device(zh=1 - me.zh, zl=jnp.where(up, 0, 3))

    barrier = pltpu.get_barrier_semaphore()
    for device in (
        me.neighbour("x", 1),
        me.neighbour("x", -1),
        me.neighbour("y", 1),
        me.neighbour("y", -1),
        partner,
    ):
        pl.semaphore_signal(barrier, inc=1, device_id=device, device_id_type=MESH)

    @pl.when(jnp.logical_not(is_source))
    def _():
        pl.semaphore_signal(barrier, inc=1, device_id=z_source, device_id_type=MESH)

    pl.semaphore_wait(barrier, 5 + 2 * jnp.logical_or(sends_up, sends_down).astype(jnp.int32))

    def z_copy(zl, half):
        return pltpu.make_async_remote_copy(
            src_ref=w_ref.at[pl.ds(half * HALF, HALF)],
            dst_ref=wbuf.at[0, pl.ds(half * HALF, HALF)],
            send_sem=wz.at[half + 2 * (0 if zl in (0, 3) else 1)],
            recv_sem=wz.at[4 + half],
            device_id=me.device(zh=1 - me.zh, zl=zl),
            device_id_type=MESH,
        )

    @pl.when(sends_up)
    def _():
        for half in (0, 1):
            for zl in (0, 1):
                z_copy(zl, half).start()

    @pl.when(sends_down)
    def _():
        for half in (0, 1):
            for zl in (3, 2):
                z_copy(zl, half).start()

    lat_own = pltpu.make_async_copy(lat_ref, latb.at[core], misc.at[0])
    lat_own.start()
    klo_own = pltpu.make_async_copy(klo_ref, klob.at[core], misc.at[1])
    klo_own.start()
    lat_away = pltpu.make_async_remote_copy(
        src_ref=lat_ref, dst_ref=latb.at[core], send_sem=misc.at[2], recv_sem=misc.at[3], device_id=partner, device_id_type=MESH
    )
    lat_away.start()
    klo_away = pltpu.make_async_remote_copy(
        src_ref=klo_ref, dst_ref=klob.at[core], send_sem=misc.at[4], recv_sem=misc.at[5], device_id=partner, device_id_type=MESH
    )
    klo_away.start()

    def group_of(step, half):
        dx, dy = gray(step % 4), gray(step // 4)
        return (((me.x + dx) % 4) * 2 + half) * 4 + (me.y + dy) % 4

    def columns(step, half, width):
        return pl.ds(pl.multiple_of(group_of(step, half) * width, width), width)

    def own_q(s):
        return pltpu.make_async_copy(q_hbm.at[:, columns(s, core, QW)], qbuf.at[s, core], loc_q.at[s])

    def own_go(s):
        return pltpu.make_async_copy(go_hbm.at[:, columns(s, core, VW)], gobuf.at[s, core], loc_go.at[s])

    def away_q(s):
        return pltpu.make_async_remote_copy(
            src_ref=q_hbm.at[:, columns(s, other, QW)],
            dst_ref=qbuf.at[s, core],
            send_sem=snd_q.at[s],
            recv_sem=rem_q.at[s],
            device_id=partner,
            device_id_type=MESH,
        )

    def away_go(s):
        return pltpu.make_async_remote_copy(
            src_ref=go_hbm.at[:, columns(s, other, VW)],
            dst_ref=gobuf.at[s, core],
            send_sem=snd_go.at[s],
            recv_sem=rem_go.at[s],
            device_id=partner,
            device_id_type=MESH,
        )

    def from_q(s):
        return pltpu.make_async_remote_copy(
            src_ref=q_hbm.at[:, columns(s, core, QW)],
            dst_ref=qbuf.at[s, other],
            send_sem=snd_q.at[s],
            recv_sem=rem_q.at[s],
            device_id=partner,
            device_id_type=MESH,
        )

    def from_go(s):
        return pltpu.make_async_remote_copy(
            src_ref=go_hbm.at[:, columns(s, core, VW)],
            dst_ref=gobuf.at[s, other],
            send_sem=snd_go.at[s],
            recv_sem=rem_go.at[s],
            device_id=partner,
            device_id_type=MESH,
        )

    def gather_copy(half, dx, dy, piece, axis, sign):
        first, count = rows_of(half, piece)
        there = (dx - sign, dy) if axis == "x" else (dx, dy - sign)
        there = (there[0] % 4, there[1] % 4)
        index = GATHER[(half, there[0], there[1], piece)]
        return pltpu.make_async_remote_copy(
            src_ref=wbuf.at[slot_of(dx, dy), pl.ds(first, count)],
            dst_ref=wbuf.at[slot_of(*there), pl.ds(first, count)],
            send_sem=ag_send.at[index],
            recv_sem=ag_recv.at[index],
            device_id=me.neighbour(axis, sign),
            device_id_type=MESH,
        )

    def gather_wait(half, dx, dy, piece):
        first, count = rows_of(half, piece)
        index = GATHER[(half, dx, dy, piece)]
        pltpu.make_async_remote_copy(
            src_ref=wbuf.at[slot_of(dx, dy), pl.ds(first, count)],
            dst_ref=wbuf.at[slot_of(dx, dy), pl.ds(first, count)],
            send_sem=ag_send.at[index],
            recv_sem=ag_recv.at[index],
            device_id=me.neighbour("x", 1),
            device_id_type=MESH,
        ).wait_recv()

    def gather_event(half, along, across):
        first_axis = main_axis(half)
        second_axis = "y" if first_axis == "x" else "x"
        dx, dy = at(first_axis, along, across)
        if along or across:
            last = across if across else along
            for piece in ("0", "1") if last == 2 else ("f",):
                gather_wait(half, dx, dy, piece)
        if across == 0:
            if along == 0:
                for sign in (1, -1):
                    gather_copy(half, dx, dy, "f", first_axis, sign).start()
            elif along == 3:
                gather_copy(half, dx, dy, "0", first_axis, 1).start()
            elif along == 1:
                gather_copy(half, dx, dy, "1", first_axis, -1).start()
            for sign in (1, -1):
                gather_copy(half, dx, dy, "f", second_axis, sign).start()
        elif across == 3:
            gather_copy(half, dx, dy, "0", second_axis, 1).start()
        elif across == 1:
            gather_copy(half, dx, dy, "1", second_axis, -1).start()

    def gather_sends():
        done = []
        for half in (0, 1):
            first_axis = main_axis(half)
            second_axis = "y" if first_axis == "x" else "x"
            for along in range(4):
                dx, dy = at(first_axis, along, 0)
                if along == 0:
                    done += [(half, dx, dy, "f", first_axis, 1), (half, dx, dy, "f", first_axis, -1)]
                elif along == 3:
                    done += [(half, dx, dy, "0", first_axis, 1)]
                elif along == 1:
                    done += [(half, dx, dy, "1", first_axis, -1)]
                done += [(half, dx, dy, "f", second_axis, 1), (half, dx, dy, "f", second_axis, -1)]
                dx, dy = at(first_axis, along, 3)
                done += [(half, dx, dy, "0", second_axis, 1)]
                dx, dy = at(first_axis, along, 1)
                done += [(half, dx, dy, "1", second_axis, -1)]
        return done

    events = {
        1: [(0, 1, 0), (0, 3, 0), (1, 1, 0), (1, 3, 0), (1, 0, 1)],
        2: [(1, 0, 3), (0, 0, 1), (0, 0, 3)],
        3: [(0, 2, 0), (1, 2, 0), (1, 0, 2)],
        4: [],
        5: [(0, 1, 1), (1, 1, 1)],
        6: [(0, 3, 1), (1, 1, 3)],
        7: [(0, 2, 1), (1, 1, 2)],
        8: [],
        9: [(0, 1, 3), (1, 3, 1)],
        10: [(0, 3, 3), (1, 3, 3)],
        11: [(0, 2, 3), (1, 3, 2)],
        12: [(0, 0, 2)],
        13: [(0, 1, 2), (1, 2, 1)],
        14: [(0, 3, 2), (1, 2, 3)],
        15: [(0, 2, 2), (1, 2, 2)],
    }

    @pl.when(is_source)
    def _():
        own = pltpu.make_async_copy(w_ref, wbuf.at[0], misc.at[6])
        own.start()
        own.wait()

    @pl.when(jnp.logical_not(is_source))
    def _():
        for half in (0, 1):
            z_copy(0, half).wait_recv()

    gather_event(0, 0, 0)
    gather_event(1, 0, 0)

    def start_tokens(s, carry):
        away_q(s).start()
        away_go(s).start()
        own_q(s).start()
        own_go(s).start()
        return carry

    lax.fori_loop(0, 16, start_tokens, 0)

    lat_own.wait()
    klo_own.wait()
    for trace in range(2):
        pass
    pltpu.make_async_remote_copy(
        src_ref=lat_ref, dst_ref=latb.at[other], send_sem=misc.at[2], recv_sem=misc.at[3], device_id=partner, device_id_type=MESH
    ).wait_recv()
    pltpu.make_async_remote_copy(
        src_ref=klo_ref, dst_ref=klob.at[other], send_sem=misc.at[4], recv_sem=misc.at[5], device_id=partner, device_id_type=MESH
    ).wait_recv()
    key = lax.broadcasted_iota(jnp.int32, (KEYS, OWN), 0)
    row = lax.broadcasted_iota(jnp.int32, (KEYS, OWN), 1)
    place = (key % STRETCH + STRETCH * (key // OWN)).astype(F32)
    latest = (STRETCH + row % STRETCH).astype(F32)
    same = ((key % OWN) // STRETCH) == (row // STRETCH)
    for trace in range(2):
        allowed = same & (place <= latest) & (place >= klob[trace, 0:1, :])
        bias[trace] = jnp.where(allowed, 0.0, -jnp.inf)
        lat_t[:, trace * KEYS : (trace + 1) * KEYS] = latb[trace, :, :D_LAT].T
    acc[...] = jnp.zeros_like(acc)

    def dot(a, b, ca=1, cb=0):
        return lax.dot_general(a, b, (((ca,), (cb,)), ((), ())), preferred_element_type=F32)

    def local_gq(s):
        return pltpu.make_async_copy(gqbuf.at[s, core], gq_hbm.at[:, columns(s, core, QW)], gq_loc.at[s])

    def away_gq(s):
        return pltpu.make_async_remote_copy(
            src_ref=gqbuf.at[s, other],
            dst_ref=gq_hbm.at[:, columns(s, core, QW)],
            send_sem=gq_snd.at[s],
            recv_sem=gq_rcv.at[s],
            device_id=partner,
            device_id_type=MESH,
        )

    def from_gq(s):
        return pltpu.make_async_remote_copy(
            src_ref=gqbuf.at[s, other],
            dst_ref=gq_hbm.at[:, columns(s, other, QW)],
            send_sem=gq_snd.at[s],
            recv_sem=gq_rcv.at[s],
            device_id=partner,
            device_id_type=MESH,
        )

    def step_body(s, carry):
        for at_step, todo in events.items():
            if todo:

                @pl.when(s == at_step)
                def _(todo=todo):
                    for event in todo:
                        gather_event(*event)

        own_q(s).wait()
        own_go(s).wait()
        from_q(s).wait_recv()
        from_go(s).wait_recv()
        for trace in range(2):
            kvbuf[trace * KEYS : (trace + 1) * KEYS, :] = dot(latb[trace, :, :D_LAT], wbuf[s]).astype(BF16)
        for trace in range(2):
            span = slice(trace * KEYS, (trace + 1) * KEYS)
            rope = latb[trace, :, D_LAT:]
            queries = qbuf[s, trace]
            grads = gobuf[s, trace]
            out = []
            grope = None
            for head in range(2):
                base = head * (D_NOPE + D_V)
                keys = jnp.concatenate([kvbuf[span, base : base + D_NOPE], rope], 1)
                values = kvbuf[span, base + D_NOPE : base + D_NOPE + D_V]
                query = queries[:, head * (D_NOPE + D_ROPE) : (head + 1) * (D_NOPE + D_ROPE)]
                grad = grads[:, head * D_V : (head + 1) * D_V]
                scores = dot(keys, query, 1, 1) * SCALE + bias[trace]
                highest = jnp.max(scores, 0, keepdims=True)
                expo = jnp.exp(scores - highest)
                probs = expo * (1.0 / jnp.sum(expo, 0, keepdims=True))
                dprob = dot(values, grad, 1, 1)
                delta = jnp.sum(probs * dprob, 0, keepdims=True)
                dscore = (probs * (dprob - delta) * SCALE).astype(BF16)
                gkey = dot(dscore, query)
                gkvbuf[span, base : base + D_NOPE] = gkey[:, :D_NOPE].astype(BF16)
                gkvbuf[span, base + D_NOPE : base + D_NOPE + D_V] = dot(probs.astype(BF16), grad).astype(BF16)
                grope = gkey[:, D_NOPE:] if grope is None else grope + gkey[:, D_NOPE:]
                out.append(dot(dscore, keys, 0, 0).astype(BF16))
            gqbuf[s, trace] = jnp.concatenate(out, 1)
            acc[trace, :, D_LAT:] += grope
        local_gq(s).start()
        away_gq(s).start()
        for trace in range(2):
            acc[trace, :, :D_LAT] += dot(gkvbuf[trace * KEYS : (trace + 1) * KEYS, :], wbuf[s], 1, 1)
        gbuf[s] = dot(lat_t[...], gkvbuf[...]).astype(BF16)
        return carry

    lax.fori_loop(0, 16, step_body, 0)

    acc_away = pltpu.make_async_remote_copy(
        src_ref=acc.at[other], dst_ref=accin, send_sem=misc.at[7], recv_sem=misc.at[8], device_id=partner, device_id_type=MESH
    )
    acc_away.start()

    def reduce_copy(half, phase, across, piece, axis, sign, dx, dy, rows, index_piece):
        first, count = rows
        index, row, _ = REDUCE[(half, phase, across, index_piece)]
        return pltpu.make_async_remote_copy(
            src_ref=gbuf.at[slot_of(dx, dy), pl.ds(first, count)],
            dst_ref=rbuf.at[pl.ds(row, count)],
            send_sem=rs_send.at[index],
            recv_sem=rs_recv.at[index],
            device_id=me.neighbour(axis, sign),
            device_id_type=MESH,
        )

    def reduce_plan(half, phase, across):
        first_axis = main_axis(half)
        second_axis = "y" if first_axis == "x" else "x"
        axis = second_axis if phase == 0 else first_axis

        def place_of(step):
            return at(first_axis, across, step) if phase == 0 else at(first_axis, step, 0)

        far, back, ahead = place_of(2), place_of(3), place_of(1)
        whole = rows_of(half, "f")
        return {
            "0": reduce_copy(half, phase, across, "0", axis, -1, *far, rows_of(half, "0"), "0"),
            "1": reduce_copy(half, phase, across, "1", axis, 1, *far, rows_of(half, "1"), "1"),
            "back": reduce_copy(half, phase, across, "f", axis, -1, *back, whole, "from1"),
            "ahead": reduce_copy(half, phase, across, "f", axis, 1, *ahead, whole, "from3"),
            "slots": (slot_of(*back), slot_of(*ahead), slot_of(*place_of(0))),
        }

    plans = {
        (half, phase, across): reduce_plan(half, phase, across)
        for half in (0, 1)
        for phase in (0, 1)
        for across in (range(4) if phase == 0 else (0,))
    }

    def add_rows(slot, first, count, sources):
        for start in range(0, count, 64):
            span = pl.ds(first + start, 64)
            total = gbuf[slot, span, :].astype(F32)
            for source in sources:
                total = total + rbuf[pl.ds(source + start, 64), :].astype(F32)
            gbuf[slot, span, :] = total.astype(BF16)

    def stage_far(half, phase, across):
        plan = plans[(half, phase, across)]
        plan["0"].start()
        plan["1"].start()

    def stage_near(half, phase, across):
        plan = plans[(half, phase, across)]
        back, ahead, _ = plan["slots"]
        for piece, slot, name in (("0", back, "back"), ("1", ahead, "ahead")):
            plan[piece].wait_recv()
            first, count = rows_of(half, piece)
            add_rows(slot, first, count, [REDUCE[(half, phase, across, piece)][1]])
            plan[name].start()

    def stage_own(half, phase, across):
        plan = plans[(half, phase, across)]
        plan["back"].wait_recv()
        plan["ahead"].wait_recv()
        first, count = rows_of(half, "f")
        own = plan["slots"][2]
        sources = [REDUCE[(half, phase, across, name)][1] for name in ("from1", "from3")]
        add_rows(own, first, count, sources)

    order = (2, 1, 3, 0)
    for across in order:
        for half in (0, 1):
            stage_far(half, 0, across)
    for across in order:
        for half in (0, 1):
            stage_near(half, 0, across)
    for across in order:
        for half in (0, 1):
            stage_own(half, 0, across)
        if across == 2:
            for half in (0, 1):
                stage_far(half, 1, 0)
    for half in (0, 1):
        stage_near(half, 1, 0)
    for half in (0, 1):
        stage_own(half, 1, 0)
    sum_ref[...] = gbuf[0]

    acc_away.wait_recv()
    for start in range(0, KEYS, 64):
        glat_ref[start : start + 64, :] = acc[core, start : start + 64, :] + accin[start : start + 64, :]

    def finish(s, carry):
        away_q(s).wait_send()
        away_go(s).wait_send()
        local_gq(s).wait()
        away_gq(s).wait_send()
        from_gq(s).wait_recv()
        return carry

    lax.fori_loop(0, 16, finish, 0)
    acc_away.wait_send()
    lat_away.wait_send()
    klo_away.wait_send()
    for args in gather_sends():
        gather_copy(*args).wait_send()
    for plan in plans.values():
        for name in ("0", "1", "back", "ahead"):
            plan[name].wait_send()

    @pl.when(sends_up)
    def _():
        for half in (0, 1):
            for zl in (0, 1):
                z_copy(zl, half).wait_send()

    @pl.when(sends_down)
    def _():
        for half in (0, 1):
            for zl in (3, 2):
                z_copy(zl, half).wait_send()


def main_call(queries, grad_out, lat, klo, weight):
    dma = pltpu.SemaphoreType.DMA
    any_spec = pl.BlockSpec(memory_space=pl.ANY)
    vmem = pl.BlockSpec(memory_space=pltpu.VMEM)
    return pl.pallas_call(
        main_kernel,
        out_shape=(
            jax.ShapeDtypeStruct(queries.shape, BF16),
            jax.ShapeDtypeStruct((KEYS, D_ALL), F32),
            jax.ShapeDtypeStruct((D_LAT, KVW), BF16),
        ),
        in_specs=[any_spec, any_spec, vmem, vmem, vmem],
        out_specs=(any_spec, vmem, vmem),
        scratch_shapes=[
            pltpu.VMEM((16, 2, OWN, QW), BF16),
            pltpu.VMEM((16, 2, OWN, VW), BF16),
            pltpu.VMEM((16, 2, OWN, QW), BF16),
            pltpu.VMEM((2, KEYS, D_ALL), BF16),
            pltpu.VMEM((D_LAT, 2 * KEYS), BF16),
            pltpu.VMEM((2, 8, OWN), F32),
            pltpu.VMEM((2, KEYS, OWN), F32),
            pltpu.VMEM((16, D_LAT, KVW), BF16),
            pltpu.VMEM((16, D_LAT, KVW), BF16),
            pltpu.VMEM((REDUCE_ROWS, KVW), BF16),
            pltpu.VMEM((2 * KEYS, KVW), BF16),
            pltpu.VMEM((2 * KEYS, KVW), BF16),
            pltpu.VMEM((2, KEYS, D_ALL), F32),
            pltpu.VMEM((KEYS, D_ALL), F32),
        ]
        + [dma((16,))] * 6
        + [dma((9,)), dma((6,))]
        + [dma((len(GATHER),))] * 2
        + [dma((len(REDUCE),))] * 2
        + [dma((16,))] * 3,
        compiler_params=pltpu.CompilerParams(collective_id=0, has_side_effects=True, vmem_limit_bytes=VMEM_LIMIT),
        cost_estimate=pl.CostEstimate(flops=16_000_000_000, bytes_accessed=12_000_000, transcendentals=2_000_000),
        name="attend",
    )(queries, grad_out, lat, klo, weight)


def z_kernel(part_ref, out_ref, parts, piece, pieces, send1, recv1, send2, recv2):
    me = Coords()
    mine = me.zh == me.core
    place = me.zh * 4 + me.zl

    barrier = pltpu.get_barrier_semaphore()
    everyone = [(zh, zl, core) for zh in (0, 1) for zl in range(4) for core in (0, 1)]
    def meets(zh, zl, core):
        same_core = core == me.core
        same_half = zh == me.zh
        itself = same_core & same_half & (zl == me.zl)
        return jnp.logical_and(jnp.logical_or(same_core, same_half), jnp.logical_not(itself))

    for zh, zl, core in everyone:

        @pl.when(meets(zh, zl, core))
        def _(zh=zh, zl=zl, core=core):
            pl.semaphore_signal(barrier, inc=1, device_id=me.device(zh=zh, zl=zl, core=core), device_id_type=MESH)

    pl.semaphore_wait(barrier, 11)

    def first(zl):
        return pltpu.make_async_remote_copy(
            src_ref=part_ref.at[pl.ds(zl * QUARTER, QUARTER)],
            dst_ref=parts.at[place],
            send_sem=send1.at[zl],
            recv_sem=recv1.at[place],
            device_id=me.device(zh=me.core, zl=zl),
            device_id_type=MESH,
        )

    for zl in range(4):

        @pl.when(jnp.logical_not(jnp.logical_and(mine, me.zl == zl)))
        def _(zl=zl):
            first(zl).start()

    def second(zl, core):
        return pltpu.make_async_remote_copy(
            src_ref=piece,
            dst_ref=pieces.at[me.zl],
            send_sem=send2.at[zl * 2 + core],
            recv_sem=recv2.at[me.zl],
            device_id=me.device(zl=zl, core=core),
            device_id_type=MESH,
        )

    def is_me(zl, core):
        return jnp.logical_and(me.zl == zl, me.core == core)

    @pl.when(mine)
    def _():
        for source in range(8):

            @pl.when(place != source)
            def _(source=source):
                pltpu.make_async_remote_copy(
                    src_ref=parts.at[source],
                    dst_ref=parts.at[source],
                    send_sem=send1.at[0],
                    recv_sem=recv1.at[source],
                    device_id=me.device(zh=me.core, zl=0),
                    device_id_type=MESH,
                ).wait_recv()

            @pl.when(place == source)
            def _(source=source):
                parts[source] = part_ref[pl.ds(pl.multiple_of(me.zl * QUARTER, QUARTER), QUARTER), :]

        for start in range(0, QUARTER, 64):
            total = parts[0, start : start + 64, :].astype(F32)
            for source in range(1, 8):
                total = total + parts[source, start : start + 64, :].astype(F32)
            piece[start : start + 64, :] = total.astype(BF16)
        for zl in range(4):
            for core in (0, 1):

                @pl.when(jnp.logical_not(is_me(zl, core)))
                def _(zl=zl, core=core):
                    second(zl, core).start()

    for zl in range(4):
        here = jnp.logical_and(mine, me.zl == zl)

        @pl.when(here)
        def _(zl=zl):
            out_ref[zl * QUARTER : (zl + 1) * QUARTER, :] = piece[...].astype(F32)

        @pl.when(jnp.logical_not(here))
        def _(zl=zl):
            pltpu.make_async_remote_copy(
                src_ref=piece,
                dst_ref=pieces.at[zl],
                send_sem=send2.at[0],
                recv_sem=recv2.at[zl],
                device_id=me.device(core=1 - me.core),
                device_id_type=MESH,
            ).wait_recv()
            out_ref[zl * QUARTER : (zl + 1) * QUARTER, :] = pieces[zl].astype(F32)

    for zl in range(4):

        @pl.when(jnp.logical_not(jnp.logical_and(mine, me.zl == zl)))
        def _(zl=zl):
            first(zl).wait_send()

        for core in (0, 1):

            @pl.when(jnp.logical_and(mine, jnp.logical_not(is_me(zl, core))))
            def _(zl=zl, core=core):
                second(zl, core).wait_send()


def z_call(part):
    dma = pltpu.SemaphoreType.DMA
    vmem = pl.BlockSpec(memory_space=pltpu.VMEM)
    return pl.pallas_call(
        z_kernel,
        out_shape=jax.ShapeDtypeStruct((D_LAT, KVW), F32),
        in_specs=[vmem],
        out_specs=vmem,
        scratch_shapes=[
            pltpu.VMEM((8, QUARTER, KVW), BF16),
            pltpu.VMEM((QUARTER, KVW), BF16),
            pltpu.VMEM((4, QUARTER, KVW), BF16),
            dma((4,)),
            dma((8,)),
            dma((8,)),
            dma((4,)),
        ],
        compiler_params=pltpu.CompilerParams(collective_id=1, has_side_effects=True, vmem_limit_bytes=VMEM_LIMIT),
        name="sum_z",
    )(part)


def spread(blocks):
    count = lax.axis_size("ctx")
    rows = STRETCH // count
    parts = blocks.reshape(2, count, rows * D_ALL).transpose(1, 0, 2)
    return lax.all_to_all(parts, "ctx", split_axis=0, concat_axis=0, tiled=True).reshape(2 * count, rows * D_ALL)


def collect(parts):
    count = lax.axis_size("ctx")
    rows = STRETCH // count
    parts = lax.all_to_all(parts.reshape(count, 2, rows * D_ALL), "ctx", split_axis=0, concat_axis=0, tiled=True)
    return parts.transpose(1, 0, 2).reshape(2 * STRETCH, D_ALL)


def per_device(queries, grad_out, latent, up_weight, doc_lengths, stretch_order):
    order = stretch_order[0]
    slots = jnp.arange(order.shape[0], dtype=jnp.int32)
    before = jnp.sum(jnp.where(order[None, :] == order[:, None] - 1, slots[None, :], 0), 1)
    after = jnp.sum(jnp.where(order[None, :] == order[:, None] + 1, slots[None, :], 0), 1)
    has_after = order < order.shape[0] - 1

    ends = jnp.cumsum(doc_lengths[0])
    starts = ends - doc_lengths[0]
    me = lax.axis_index("ctx")
    mine = lax.dynamic_slice_in_dim(order, 2 * me, 2)
    position = (mine[:, None] * STRETCH + jnp.arange(STRETCH, dtype=jnp.int32)[None, :]).reshape(OWN)
    start = jnp.max(jnp.where(starts[:, None] <= position[None, :], starts[:, None], 0), 0)
    klo = (start - jnp.repeat(mine, STRETCH) * STRETCH + STRETCH).astype(F32)
    klo = jnp.broadcast_to(klo[None, :], (8, OWN))

    own = latent[0]
    halo = collect(jnp.take(spread(own.reshape(2, STRETCH, D_ALL)), before, axis=0))
    lat = jnp.concatenate([halo, own], 0)
    gq, glat, part = main_call(queries[0], grad_out[0], lat, klo, up_weight)
    weight_grad = z_call(part)

    returned = jnp.take(spread(glat[:OWN].astype(BF16).reshape(2, STRETCH, D_ALL)), after, axis=0)
    returned = collect(jnp.where(has_after[:, None], returned, jnp.zeros_like(returned)))
    latent_grad = (glat[OWN:] + returned.astype(F32)).astype(BF16)
    return gq[None], latent_grad[None], weight_grad


def solution(mesh):
    in_specs = (
        P("dp", "ctx", None),
        P("dp", "ctx", None),
        P("dp", "ctx", None),
        P(None, "ctx"),
        P("dp", None),
        P("dp", None),
    )
    out_specs = (P("dp", "ctx", None), P("dp", "ctx", None), P(None, "ctx"))
    return jax.shard_map(per_device, mesh=mesh, in_specs=in_specs, out_specs=out_specs, check_vma=False)
```

time: 1010 us -> 253 us (0.25)
  the two profiles are of different devices: /device:TPU:64 before, /device:TPU:1 now
where the time goes in v1:
time: 253 us; the launch traced here: 251 us
  Pallas kernels  172 us (68%)
  waiting for transfers between devices  30.1 us (12%)
  starting transfers between devices  27.6 us (11%)
  local copies, waits for them, and re-layouts  14.9 us (6%)
  other arithmetic  5.53 us (2%)
    pallas_call x1, Pallas kernels, main_call(): pl.pallas_call(main_kernel, out_shape=(jax.ShapeDtypeStruct(queries.shape...  131 us
    pallas_call x1, Pallas kernels, z_call(): pl.pallas_call(z_kernel, out_shape=jax.ShapeDtypeStruct((D_LAT, KVW), F32...  41 us
    all_to_all x2, starting transfers between devices, spread(): lax.all_to_all(parts, 'ctx', split_axis=0, concat_axis=0, tiled=True)  19.3 us
    all_to_all x2, waiting for transfers between devices, spread(): lax.all_to_all(parts, 'ctx', split_axis=0, concat_axis=0, tiled=True)  18.7 us
    all_to_all x2, waiting for transfers between devices, collect(): lax.all_to_all(parts.reshape(count, 2, rows * D_ALL), 'ctx', split_axis=0...  11.4 us
    all_to_all x2, starting transfers between devices, collect(): lax.all_to_all(parts.reshape(count, 2, rows * D_ALL), 'ctx', split_axis=0...  8.3 us
  transfers between devices with their start and end apart: 4, of which 3 were waited for; matrix products, arithmetic and copies ran while one was open for 2% of the time, Pallas kernels for 16%

profile of v1, /device:TPU:1, one launch (start us, length us, event | category | flops | bytes accessed | tf_op | source)
XLA Modules:
  0.0 251.4 jit_solution(4151617912384862658)
XLA Ops:
  0.6 1.1 copy.31
  1.7 0.2 reshape_reshape_squeeze.3
  1.9 0.8 copy.32
  2.6 14.5 %all-to-all-start = ((bf16[32,2,1152]{2,1,0:T(2,128)(2,1)}), bf16[32,2,1152]{2,1,0:T(2,128)(2,1)S(1)}, u32[]{:S(2)}, u32[]{:S(2)}) async-start(bf16[32,2,1152]{2,1,0:T(2,128)(2,1)} %copy.32), calls=%async_computation | async-start | bytes 294912 | tf_op jit(solution)/shard_map/all_to_all | solution.py:778
  17.1 0.7 broadcast_add_fusion.1
  17.8 0.8 select_reduce_fusion.1
  18.7 0.7 multiply_bitcast_fusion
  19.4 0.1 iota_add_fusion
  19.5 0.1 add.57
  19.6 0.8 copy.35
  20.3 0.2 reduce-window.8
  20.5 0.1 reduce
  20.6 0.1 add.54
  20.7 0.1 mul.23
  20.8 0.7 bitcast_subtract_fusion
  21.4 7.2 %all-to-all-done = bf16[32,2,1152]{2,1,0:T(2,128)(2,1)S(1)} async-done(((bf16[32,2,1152]{2,1,0:T(2,128)(2,1)}), bf16[32,2,1152]{2,1,0:T(2,128)(2,1)S(1)}, u32[]{:S(2)}, u32[]{:S(2)}) %all-to-all-start) | async-done | bytes 147488 | tf_op jit(solution)/shard_map/all_to_all | solution.py:778
  28.6 0.1 reshape.119
  28.7 0.7 gather_fusion
  29.4 0.1 broadcast_select_fusion
  29.5 0.7 reshape.120
  30.3 4.4 %all-to-all-start.1 = ((bf16[32,2,1152]{2,1,0:T(2,128)(2,1)}), bf16[32,2,1152]{2,1,0:T(2,128)(2,1)S(1)}, u32[]{:S(2)}, u32[]{:S(2)}) async-start(bf16[32,2,1152]{2,1,0:T(2,128)(2,1)} %reshape.120), calls=%async_computation.1 | async-start | bytes 294912 | tf_op jit(solution)/shard_map/all_to_all | solution.py:784
  34.7 0.1 select_reduce_fusion
  34.8 11.4 %all-to-all-done.1 = bf16[32,2,1152]{2,1,0:T(2,128)(2,1)S(1)} async-done(((bf16[32,2,1152]{2,1,0:T(2,128)(2,1)}), bf16[32,2,1152]{2,1,0:T(2,128)(2,1)S(1)}, u32[]{:S(2)}, u32[]{:S(2)}) %all-to-all-start.1) | async-done | bytes 147488 | tf_op jit(solution)/shard_map/all_to_all | solution.py:784
  46.3 0.1 reshape.121
  46.4 0.8 pad_maximum_fusion.lat_ref
  47.2 0.6 broadcast_in_dim.71.klo_ref
  47.8 131.3 %attend.1 = (bf16[128,12288]{1,0:T(8,128)(2,1)}, f32[256,576]{1,0:T(8,128)}, bf16[512,512]{1,0:T(8,128)(2,1)}) custom-call(bf16[128,12288]{1,0:T(8,128)(2,1)} %bitcast.27, bf16[128,8192]{1,0:T(8,128)(2,1)} %bitcast.28, bf16[256,576]{1,0:T(8,128)(2,1)} %pad_maximum_fusion.lat_ref, f32[8,128]{1,0:T(8,128)} %broadcast_in_dim.71.klo_ref, bf16[512,512]{1,0:T(8,128)(2,1)} %w_ref.1), custom_call_target="tpu_custom_call" | custom-call | flops 16000000000 | bytes 12000000 | tf_op jit(solution)/shard_map/attend/pallas_call | solution.py:603
  179.1 1.0 slice.18
  180.1 0.1 reshape_reshape.3
  180.3 0.8 copy.36
  181.0 4.8 %all-to-all-start.2 = ((bf16[32,2,1152]{2,1,0:T(2,128)(2,1)}), bf16[32,2,1152]{2,1,0:T(2,128)(2,1)S(1)}, u32[]{:S(2)}, u32[]{:S(2)}) async-start(bf16[32,2,1152]{2,1,0:T(2,128)(2,1)} %copy.36), calls=%async_computation.2 | async-start | bytes 294912 | tf_op jit(solution)/shard_map/all_to_all | solution.py:778
  185.9 11.5 %all-to-all-done.2 = bf16[32,2,1152]{2,1,0:T(2,128)(2,1)S(1)} async-done(((bf16[32,2,1152]{2,1,0:T(2,128)(2,1)}), bf16[32,2,1152]{2,1,0:T(2,128)(2,1)S(1)}, u32[]{:S(2)}, u32[]{:S(2)}) %all-to-all-start.2) | async-done | bytes 147488 | tf_op jit(solution)/shard_map/all_to_all | solution.py:778
  197.4 0.1 reshape.125
  197.5 0.0 copy-start.1
  197.5 0.7 gather_fusion.1
  198.2 0.1 select_select_fusion
  198.3 0.7 reshape.126
  199.0 3.9 %all-to-all-start.3 = ((bf16[32,2,1152]{2,1,0:T(2,128)(2,1)}), bf16[32,2,1152]{2,1,0:T(2,128)(2,1)S(1)}, u32[]{:S(2)}, u32[]{:S(2)}) async-start(bf16[32,2,1152]{2,1,0:T(2,128)(2,1)} %reshape.126), calls=%async_computation.3 | async-start | bytes 294912 | tf_op jit(solution)/shard_map/all_to_all | solution.py:784
  202.9 41.0 %sum_z.1 = f32[512,512]{1,0:T(8,128)} custom-call(bf16[512,512]{1,0:T(8,128)(2,1)} %get-tuple-element.9.part_ref), custom_call_target="tpu_custom_call" | custom-call | tf_op jit(solution)/shard_map/sum_z/pallas_call | solution.py:755
  243.9 0.0 all-to-all-done.3
  243.9 0.1 convert_bitcast_fusion
  244.0 0.7 copy.37
  244.8 1.8 reshape.127
  246.6 1.1 fusion
  247.7 0.8 copy.38
  248.5 1.7 copy.41
  250.1 0.3 copy-done
  250.4 1.0 copy.42
  (12 shorter events, 0.1 us)
Async XLA Ops:
  2.6 26.0 %all-to-all-start = ((bf16[32,2,1152]{2,1,0:T(2,128)(2,1)}), bf16[32,2,1152]{2,1,0:T(2,128)(2,1)S(1)}, u32[]{:S(2)}, u32[]{:S(2)}) async-start(bf16[32,2,1152]{2,1,0:T(2,128)(2,1)} %copy.32), calls=%async_computation | async-start | bytes 294912 | tf_op jit(solution)/shard_map/all_to_all | solution.py:778
  30.3 16.0 %all-to-all-start.1 = ((bf16[32,2,1152]{2,1,0:T(2,128)(2,1)}), bf16[32,2,1152]{2,1,0:T(2,128)(2,1)S(1)}, u32[]{:S(2)}, u32[]{:S(2)}) async-start(bf16[32,2,1152]{2,1,0:T(2,128)(2,1)} %reshape.120), calls=%async_computation.1 | async-start | bytes 294912 | tf_op jit(solution)/shard_map/all_to_all | solution.py:784
  47.8 138.1 %copy-start.2 = (s32[1,64]{1,0:T(1,128)S(1)}, s32[1,64]{1,0:T(1,128)}, u32[]{:S(2)}) copy-start(s32[1,64]{1,0:T(1,128)} %param.13) | copy-start | bytes 772
  181.0 16.4 %all-to-all-start.2 = ((bf16[32,2,1152]{2,1,0:T(2,128)(2,1)}), bf16[32,2,1152]{2,1,0:T(2,128)(2,1)S(1)}, u32[]{:S(2)}, u32[]{:S(2)}) async-start(bf16[32,2,1152]{2,1,0:T(2,128)(2,1)} %copy.36), calls=%async_computation.2 | async-start | bytes 294912 | tf_op jit(solution)/shard_map/all_to_all | solution.py:778
  197.5 51.0 %copy-start.1 = (bf16[128,12288]{1,0:T(8,128)(2,1)S(1)}, bf16[128,12288]{1,0:T(8,128)(2,1)}, u32[]{:S(2)}) copy-start(bf16[128,12288]{1,0:T(8,128)(2,1)} %get-tuple-element.7) | copy-start | bytes 9437188
  199.0 44.9 %all-to-all-start.3 = ((bf16[32,2,1152]{2,1,0:T(2,128)(2,1)}), bf16[32,2,1152]{2,1,0:T(2,128)(2,1)S(1)}, u32[]{:S(2)}, u32[]{:S(2)}) async-start(bf16[32,2,1152]{2,1,0:T(2,128)(2,1)} %reshape.126), calls=%async_computation.3 | async-start | bytes 294912 | tf_op jit(solution)/shard_map/all_to_all | solution.py:784
  248.5 2.0 copy-start

commit v2 on v1

v2 whole, which is shorter than its diff:
```python
import jax
import jax.numpy as jnp
from jax import lax
from jax.experimental import pallas as pl
from jax.experimental.pallas import tpu as pltpu
from jax.sharding import PartitionSpec as P


BF16 = jnp.bfloat16
F32 = jnp.float32
MESH = pl.DeviceIdType.MESH

D_NOPE = 128
D_ROPE = 64
D_V = 128
D_LAT = 512
D_ALL = D_LAT + D_ROPE
STRETCH = 64
CUT = D_ALL // 8
OWN = 128
KEYS = 256
QW = 2 * (D_NOPE + D_ROPE)
VW = 2 * D_V
KVW = 2 * (D_NOPE + D_V)
SCALE = (D_NOPE + D_ROPE) ** -0.5
HALF = D_LAT // 2
QUARTER = D_LAT // 4
VMEM_LIMIT = 60 * 1024 * 1024


ORDER = [
    (1, 0), (0, 1), (1, 1), (1, 3), (3, 1), (2, 1), (1, 2), (2, 0),
    (0, 2), (2, 3), (3, 2), (2, 2), (3, 3), (3, 0), (0, 3), (0, 0),
]
OWN_SLOT = ORDER.index((0, 0))


def slot_of(dx, dy):
    return ORDER.index((dx % 4, dy % 4))


def pick(step, digits):
    low = sum(d * 4**i for i, d in enumerate(digits[:8]))
    high = sum(d * 4**i for i, d in enumerate(digits[8:]))
    return lax.shift_right_logical(jnp.where(step < 8, low, high), 2 * (step % 8)) % 4


def rows_of(half, piece):
    base = half * HALF
    if piece == "f":
        return base, HALF
    return base + int(piece) * QUARTER, QUARTER


def main_axis(half):
    return "x" if half == 0 else "y"


def at(axis, along, across):
    return (along, across) if axis == "x" else (across, along)


class Coords:
    def __init__(self):
        dp, ctx = lax.axis_index("dp"), lax.axis_index("ctx")
        self.dp, self.ctx = dp, ctx
        self.zl, self.core = dp // 2, dp % 2
        self.x, self.zh, self.y = ctx // 8, (ctx // 4) % 2, ctx % 4

    def device(self, x=None, y=None, zh=None, zl=None, core=None):
        x = self.x if x is None else x
        y = self.y if y is None else y
        zh = self.zh if zh is None else zh
        zl = self.zl if zl is None else zl
        core = self.core if core is None else core
        return (zl * 2 + core, (x * 2 + zh) * 4 + y)

    def neighbour(self, axis, sign):
        if axis == "x":
            return self.device(x=(self.x + 4 + sign) % 4)
        return self.device(y=(self.y + 4 + sign) % 4)


def gather_keys():
    keys = []
    for half in (0, 1):
        axis = main_axis(half)
        for across in range(4):
            for along in range(4):
                dx, dy = at(axis, along, across)
                if along == 0 and across == 0:
                    continue
                last = across if across else along
                for piece in ("0", "1") if last == 2 else ("f",):
                    keys.append((half, dx, dy, piece))
    return {key: i for i, key in enumerate(keys)}


GATHER = gather_keys()


def reduce_keys():
    keys, row = {}, 0
    for half in (0, 1):
        for across in range(4):
            for phase in (0, 1):
                if phase == 1 and across:
                    continue
                for piece, count in (("0", QUARTER), ("1", QUARTER), ("from1", HALF), ("from3", HALF)):
                    keys[(half, phase, across, piece)] = (len(keys), row, count)
                    row += count
    return keys, row


REDUCE, REDUCE_ROWS = reduce_keys()


def main_kernel(
    q_hbm,
    go_hbm,
    lat_ref,
    klo_ref,
    moves_ref,
    w_ref,
    gq_hbm,
    glat_ref,
    weight_ref,
    qbuf,
    gobuf,
    gqbuf,
    latb,
    lat_t,
    klob,
    bias,
    wbuf,
    gbuf,
    rbuf,
    kvbuf,
    gkvbuf,
    acc,
    accin,
    hb0,
    hb1,
    hb2,
    hb3,
    hb4,
    hb5,
    hb6,
    hb7,
    parts,
    pieces,
    loc_q,
    loc_go,
    rem_q,
    rem_go,
    snd_q,
    snd_go,
    misc,
    lat_sem,
    hsem,
    z_send,
    z_recv,
    wz,
    ag_send,
    ag_recv,
    rs_send,
    rs_recv,
    gq_loc,
    gq_snd,
    gq_rcv,
):
    me = Coords()
    core, other = me.core, 1 - me.core
    partner = me.device(core=other)
    is_source = me.zh == core
    sends_up = jnp.logical_and(is_source, me.zl == 3)
    sends_down = jnp.logical_and(is_source, me.zl == 0)
    place = me.zh * 4 + me.zl

    def ctx_device(away):
        return (me.dp, (me.ctx + away) % 32)

    barrier = pltpu.get_barrier_semaphore()

    def greet(away, carry):
        pl.semaphore_signal(barrier, inc=1, device_id=ctx_device(away), device_id_type=MESH)
        return carry

    lax.fori_loop(1, 32, greet, 0)
    for away in (1, 2, 3):
        for zh in (me.zh, 1 - me.zh):
            pl.semaphore_signal(
                barrier, inc=1, device_id=me.device(zh=zh, zl=(me.zl + away) % 4), device_id_type=MESH
            )
    pl.semaphore_signal(barrier, inc=1, device_id=partner, device_id_type=MESH)
    pl.semaphore_wait(barrier, 38)

    def z_copy(zl, half):
        return pltpu.make_async_remote_copy(
            src_ref=w_ref.at[pl.ds(half * HALF, HALF)],
            dst_ref=wbuf.at[OWN_SLOT, pl.ds(half * HALF, HALF)],
            send_sem=wz.at[half + 2 * (0 if zl in (0, 3) else 1)],
            recv_sem=wz.at[4 + half],
            device_id=me.device(zh=1 - me.zh, zl=zl),
            device_id_type=MESH,
        )

    @pl.when(sends_up)
    def _():
        for half in (0, 1):
            for zl in (0, 1):
                z_copy(zl, half).start()

    @pl.when(sends_down)
    def _():
        for half in (0, 1):
            for zl in (3, 2):
                z_copy(zl, half).start()

    def lat_copy(trace, first):
        index = 2 if first else 0
        return pltpu.make_async_remote_copy(
            src_ref=latb.at[trace, pl.ds(first, OWN)],
            dst_ref=latb.at[trace, pl.ds(first, OWN)],
            send_sem=lat_sem.at[index],
            recv_sem=lat_sem.at[index + 1],
            device_id=partner,
            device_id_type=MESH,
        )

    def klo_copy(trace):
        return pltpu.make_async_remote_copy(
            src_ref=klo_ref,
            dst_ref=klob.at[trace],
            send_sem=misc.at[4],
            recv_sem=misc.at[5],
            device_id=partner,
            device_id_type=MESH,
        )

    def group_of(step, half):
        dx, dy = pick(step, [d[0] for d in ORDER]), pick(step, [d[1] for d in ORDER])
        return (((me.x + dx) % 4) * 2 + half) * 4 + (me.y + dy) % 4

    def columns(step, half, width):
        return pl.ds(pl.multiple_of(group_of(step, half) * width, width), width)

    def own_q(s):
        return pltpu.make_async_copy(q_hbm.at[:, columns(s, core, QW)], qbuf.at[s, core], loc_q.at[s])

    def own_go(s):
        return pltpu.make_async_copy(go_hbm.at[:, columns(s, core, VW)], gobuf.at[s, core], loc_go.at[s])

    def away_q(s):
        return pltpu.make_async_remote_copy(
            src_ref=q_hbm.at[:, columns(s, other, QW)],
            dst_ref=qbuf.at[s, core],
            send_sem=snd_q.at[s],
            recv_sem=rem_q.at[s],
            device_id=partner,
            device_id_type=MESH,
        )

    def away_go(s):
        return pltpu.make_async_remote_copy(
            src_ref=go_hbm.at[:, columns(s, other, VW)],
            dst_ref=gobuf.at[s, core],
            send_sem=snd_go.at[s],
            recv_sem=rem_go.at[s],
            device_id=partner,
            device_id_type=MESH,
        )

    def from_q(s):
        return pltpu.make_async_remote_copy(
            src_ref=q_hbm.at[:, columns(s, core, QW)],
            dst_ref=qbuf.at[s, other],
            send_sem=snd_q.at[s],
            recv_sem=rem_q.at[s],
            device_id=partner,
            device_id_type=MESH,
        )

    def from_go(s):
        return pltpu.make_async_remote_copy(
            src_ref=go_hbm.at[:, columns(s, core, VW)],
            dst_ref=gobuf.at[s, other],
            send_sem=snd_go.at[s],
            recv_sem=rem_go.at[s],
            device_id=partner,
            device_id_type=MESH,
        )

    def gather_copy(half, dx, dy, piece, axis, sign):
        first, count = rows_of(half, piece)
        there = (dx - sign, dy) if axis == "x" else (dx, dy - sign)
        there = (there[0] % 4, there[1] % 4)
        index = GATHER[(half, there[0], there[1], piece)]
        return pltpu.make_async_remote_copy(
            src_ref=wbuf.at[slot_of(dx, dy), pl.ds(first, count)],
            dst_ref=wbuf.at[slot_of(*there), pl.ds(first, count)],
            send_sem=ag_send.at[index],
            recv_sem=ag_recv.at[index],
            device_id=me.neighbour(axis, sign),
            device_id_type=MESH,
        )

    def gather_wait(half, dx, dy, piece):
        first, count = rows_of(half, piece)
        index = GATHER[(half, dx, dy, piece)]
        pltpu.make_async_remote_copy(
            src_ref=wbuf.at[slot_of(dx, dy), pl.ds(first, count)],
            dst_ref=wbuf.at[slot_of(dx, dy), pl.ds(first, count)],
            send_sem=ag_send.at[index],
            recv_sem=ag_recv.at[index],
            device_id=me.neighbour("x", 1),
            device_id_type=MESH,
        ).wait_recv()

    def gather_event(half, along, across):
        first_axis = main_axis(half)
        second_axis = "y" if first_axis == "x" else "x"
        dx, dy = at(first_axis, along, across)
        if along or across:
            last = across if across else along
            for piece in ("0", "1") if last == 2 else ("f",):
                gather_wait(half, dx, dy, piece)
        if across == 0:
            if along == 0:
                for sign in (1, -1):
                    gather_copy(half, dx, dy, "f", first_axis, sign).start()
            elif along == 3:
                gather_copy(half, dx, dy, "0", first_axis, 1).start()
            elif along == 1:
                gather_copy(half, dx, dy, "1", first_axis, -1).start()
            for sign in (1, -1):
                gather_copy(half, dx, dy, "f", second_axis, sign).start()
        elif across == 3:
            gather_copy(half, dx, dy, "0", second_axis, 1).start()
        elif across == 1:
            gather_copy(half, dx, dy, "1", second_axis, -1).start()

    def gather_sends():
        done = []
        for half in (0, 1):
            first_axis = main_axis(half)
            second_axis = "y" if first_axis == "x" else "x"
            for along in range(4):
                dx, dy = at(first_axis, along, 0)
                if along == 0:
                    done += [(half, dx, dy, "f", first_axis, 1), (half, dx, dy, "f", first_axis, -1)]
                elif along == 3:
                    done += [(half, dx, dy, "0", first_axis, 1)]
                elif along == 1:
                    done += [(half, dx, dy, "1", first_axis, -1)]
                done += [(half, dx, dy, "f", second_axis, 1), (half, dx, dy, "f", second_axis, -1)]
                dx, dy = at(first_axis, along, 3)
                done += [(half, dx, dy, "0", second_axis, 1)]
                dx, dy = at(first_axis, along, 1)
                done += [(half, dx, dy, "1", second_axis, -1)]
        return done

    events = {
        0: [(0, 1, 0), (0, 3, 0), (1, 1, 0), (1, 3, 0), (1, 0, 1)],
        1: [(0, 0, 1), (1, 0, 3), (0, 0, 3)],
        2: [(0, 2, 0), (1, 2, 0), (0, 1, 1), (1, 1, 1)],
        3: [(0, 1, 3), (1, 3, 1)],
        4: [(0, 3, 1), (1, 1, 3)],
        5: [(0, 2, 1), (1, 1, 2), (0, 3, 3), (1, 3, 3)],
        6: [(0, 1, 2), (1, 2, 1)],
        7: [(1, 0, 2), (0, 2, 3), (1, 2, 3)],
        8: [(0, 0, 2)],
        9: [(1, 3, 2)],
        10: [(0, 3, 2)],
        11: [(0, 2, 2), (1, 2, 2)],
    }

    def round_copy(source, dest, sems, away):
        to = (me.ctx + away) % 32
        return pltpu.make_async_remote_copy(
            src_ref=source.at[pl.ds(2 * to, 2)],
            dst_ref=dest.at[pl.ds(2 * me.ctx, 2)],
            send_sem=sems[0].at[away],
            recv_sem=sems[1].at[away],
            device_id=ctx_device(away),
            device_id_type=MESH,
        )

    def round_start(source, dest, sems):
        def go(away, carry):
            round_copy(source, dest, sems, away).start()
            return carry

        lax.fori_loop(1, 32, go, 0)
        for t in range(2):
            dest[2 * me.ctx + t] = source[2 * me.ctx + t]

    def round_wait(source, dest, sems):
        def go(away, carry):
            frm = (me.ctx + 32 - away) % 32
            pltpu.make_async_remote_copy(
                src_ref=source.at[pl.ds(2 * frm, 2)],
                dst_ref=dest.at[pl.ds(2 * frm, 2)],
                send_sem=sems[0].at[away],
                recv_sem=sems[1].at[away],
                device_id=ctx_device(away),
                device_id_type=MESH,
            ).wait_recv()
            return carry

        lax.fori_loop(1, 32, go, 0)

    def round_end(source, dest, sems):
        def go(away, carry):
            round_copy(source, dest, sems, away).wait_send()
            return carry

        lax.fori_loop(1, 32, go, 0)

    def cut(read, dest):
        for i in range(4):
            for t in range(2):
                rows = read(t * STRETCH + 16 * i, 16)
                for j in range(8):
                    dest[2 * (8 * i + j) + t] = rows[:, CUT * j : CUT * (j + 1)]

    def join(source, t, i):
        return jnp.concatenate([source[2 * (8 * i + j) + t] for j in range(8)], 1)

    hbuf = (hb0, hb1, hb2, hb3, hb4, hb5, hb6, hb7)
    rounds = [(hsem.at[2 * i], hsem.at[2 * i + 1]) for i in range(4)]
    cut(lambda first, count: lat_ref[first : first + count, :], hb0)
    round_start(hb0, hb1, rounds[0])

    latb[core, OWN:, :] = lat_ref[...]
    lat_copy(core, OWN).start()
    klob[core] = klo_ref[...]
    klo_copy(core).start()

    @pl.when(is_source)
    def _():
        wbuf[OWN_SLOT] = w_ref[...]

    @pl.when(jnp.logical_not(is_source))
    def _():
        for half in (0, 1):
            z_copy(0, half).wait_recv()

    gather_event(0, 0, 0)
    gather_event(1, 0, 0)

    def start_tokens(s, carry):
        away_q(s).start()
        away_go(s).start()
        own_q(s).start()
        own_go(s).start()
        return carry

    lax.fori_loop(0, 16, start_tokens, 0)

    round_wait(hb0, hb1, rounds[0])
    for s in range(64):
        hb2[s] = hb1[moves_ref[0, s]]
    round_start(hb2, hb3, rounds[1])

    klo_copy(other).wait_recv()
    key = lax.broadcasted_iota(jnp.int32, (KEYS, OWN), 0)
    row = lax.broadcasted_iota(jnp.int32, (KEYS, OWN), 1)
    spot = (key % STRETCH + STRETCH * (key // OWN)).astype(F32)
    latest = (STRETCH + row % STRETCH).astype(F32)
    same = ((key % OWN) // STRETCH) == (row // STRETCH)
    for trace in range(2):
        allowed = same & (spot <= latest) & (spot >= klob[trace, 0:1, :])
        bias[trace] = jnp.where(allowed, 0.0, -jnp.inf)
    acc[...] = jnp.zeros_like(acc)

    round_wait(hb2, hb3, rounds[1])
    for t in range(2):
        for i in range(4):
            first = t * STRETCH + 16 * i
            latb[core, first : first + 16, :] = join(hb3, t, i)
    lat_copy(core, 0).start()
    lat_copy(other, OWN).wait_recv()
    lat_copy(other, 0).wait_recv()
    for trace in range(2):
        lat_t[:, trace * KEYS : (trace + 1) * KEYS] = latb[trace, :, :D_LAT].T

    def dot(a, b, ca=1, cb=0):
        return lax.dot_general(a, b, (((ca,), (cb,)), ((), ())), preferred_element_type=F32)

    def local_gq(s):
        return pltpu.make_async_copy(gqbuf.at[s, core], gq_hbm.at[:, columns(s, core, QW)], gq_loc.at[s])

    def away_gq(s):
        return pltpu.make_async_remote_copy(
            src_ref=gqbuf.at[s, other],
            dst_ref=gq_hbm.at[:, columns(s, core, QW)],
            send_sem=gq_snd.at[s],
            recv_sem=gq_rcv.at[s],
            device_id=partner,
            device_id_type=MESH,
        )

    def from_gq(s):
        return pltpu.make_async_remote_copy(
            src_ref=gqbuf.at[s, other],
            dst_ref=gq_hbm.at[:, columns(s, other, QW)],
            send_sem=gq_snd.at[s],
            recv_sem=gq_rcv.at[s],
            device_id=partner,
            device_id_type=MESH,
        )

    def reduce_copy(half, phase, across, piece, axis, sign, dx, dy, rows, index_piece):
        first, count = rows
        index, row, _ = REDUCE[(half, phase, across, index_piece)]
        return pltpu.make_async_remote_copy(
            src_ref=gbuf.at[slot_of(dx, dy), pl.ds(first, count)],
            dst_ref=rbuf.at[pl.ds(row, count)],
            send_sem=rs_send.at[index],
            recv_sem=rs_recv.at[index],
            device_id=me.neighbour(axis, sign),
            device_id_type=MESH,
        )

    def reduce_plan(half, phase, across):
        first_axis = main_axis(half)
        second_axis = "y" if first_axis == "x" else "x"
        axis = second_axis if phase == 0 else first_axis

        def place_of(step):
            return at(first_axis, across, step) if phase == 0 else at(first_axis, step, 0)

        far, back, ahead = place_of(2), place_of(3), place_of(1)
        whole = rows_of(half, "f")
        return {
            "0": reduce_copy(half, phase, across, "0", axis, -1, *far, rows_of(half, "0"), "0"),
            "1": reduce_copy(half, phase, across, "1", axis, 1, *far, rows_of(half, "1"), "1"),
            "back": reduce_copy(half, phase, across, "f", axis, -1, *back, whole, "from1"),
            "ahead": reduce_copy(half, phase, across, "f", axis, 1, *ahead, whole, "from3"),
            "slots": (slot_of(*back), slot_of(*ahead), slot_of(*place_of(0))),
        }

    plans = {
        (half, phase, across): reduce_plan(half, phase, across)
        for half in (0, 1)
        for phase in (0, 1)
        for across in (range(4) if phase == 0 else (0,))
    }

    def add_rows(slot, first, count, sources):
        def go(i, carry):
            start = pl.multiple_of(i * 32, 32)
            span = pl.ds(first + start, 32)
            total = gbuf[slot, span, :].astype(F32)
            for source in sources:
                total = total + rbuf[pl.ds(source + start, 32), :].astype(F32)
            gbuf[slot, span, :] = total.astype(BF16)
            return carry

        lax.fori_loop(0, count // 32, go, 0)

    def stage_far(half, phase, across):
        plan = plans[(half, phase, across)]
        plan["0"].start()
        plan["1"].start()

    def stage_near(half, phase, across):
        plan = plans[(half, phase, across)]
        back, ahead, _ = plan["slots"]
        for piece, slot, name in (("0", back, "back"), ("1", ahead, "ahead")):
            plan[piece].wait_recv()
            first, count = rows_of(half, piece)
            add_rows(slot, first, count, [REDUCE[(half, phase, across, piece)][1]])
            plan[name].start()

    def stage_own(half, phase, across):
        plan = plans[(half, phase, across)]
        plan["back"].wait_recv()
        plan["ahead"].wait_recv()
        first, count = rows_of(half, "f")
        own = plan["slots"][2]
        sources = [REDUCE[(half, phase, across, name)][1] for name in ("from1", "from3")]
        add_rows(own, first, count, sources)

    sums = {
        5: [(stage_far, 1, 1)],
        6: [(stage_far, 0, 1)],
        7: [(stage_far, 1, 0), (stage_near, 1, 1)],
        8: [(stage_far, 0, 0), (stage_near, 0, 1)],
        9: [(stage_far, 1, 3), (stage_own, 1, 1)],
        10: [(stage_far, 0, 3), (stage_own, 0, 1)],
        11: [(stage_far, 0, 2), (stage_far, 1, 2)],
        12: [(stage_near, 1, 3), (stage_near, 0, 3)],
        13: [(stage_near, 0, 2), (stage_near, 1, 2), (stage_near, 1, 0)],
        14: [(stage_near, 0, 0), (stage_own, 0, 3), (stage_own, 1, 3)],
    }

    def step_body(s, carry):
        for at_step, todo in events.items():
            if todo:

                @pl.when(s == at_step)
                def _(todo=todo):
                    for event in todo:
                        gather_event(*event)

        own_q(s).wait()
        own_go(s).wait()
        from_q(s).wait_recv()
        from_go(s).wait_recv()
        for trace in range(2):
            kvbuf[trace * KEYS : (trace + 1) * KEYS, :] = dot(latb[trace, :, :D_LAT], wbuf[s]).astype(BF16)
        for trace in range(2):
            span = slice(trace * KEYS, (trace + 1) * KEYS)
            rope = latb[trace, :, D_LAT:]
            queries = qbuf[s, trace]
            grads = gobuf[s, trace]
            out = []
            grope = None
            for head in range(2):
                base = head * (D_NOPE + D_V)
                keys = jnp.concatenate([kvbuf[span, base : base + D_NOPE], rope], 1)
                values = kvbuf[span, base + D_NOPE : base + D_NOPE + D_V]
                query = queries[:, head * (D_NOPE + D_ROPE) : (head + 1) * (D_NOPE + D_ROPE)]
                grad = grads[:, head * D_V : (head + 1) * D_V]
                scores = dot(keys, query, 1, 1) * SCALE + bias[trace]
                highest = jnp.max(scores, 0, keepdims=True)
                expo = jnp.exp(scores - highest)
                probs = expo * (1.0 / jnp.sum(expo, 0, keepdims=True))
                dprob = dot(values, grad, 1, 1)
                delta = jnp.sum(probs * dprob, 0, keepdims=True)
                dscore = (probs * (dprob - delta) * SCALE).astype(BF16)
                gkey = dot(dscore, query)
                gkvbuf[span, base : base + D_NOPE] = gkey[:, :D_NOPE].astype(BF16)
                gkvbuf[span, base + D_NOPE : base + D_NOPE + D_V] = dot(probs.astype(BF16), grad).astype(BF16)
                grope = gkey[:, D_NOPE:] if grope is None else grope + gkey[:, D_NOPE:]
                out.append(dot(dscore, keys, 0, 0).astype(BF16))
            gqbuf[s, trace] = jnp.concatenate(out, 1)
            acc[trace, :, D_LAT:] += grope
        local_gq(s).start()
        away_gq(s).start()
        for trace in range(2):
            acc[trace, :, :D_LAT] += dot(gkvbuf[trace * KEYS : (trace + 1) * KEYS, :], wbuf[s], 1, 1)
        gbuf[s] = dot(lat_t[...], gkvbuf[...]).astype(BF16)
        for at_step, todo in sums.items():

            @pl.when(s == at_step)
            def _(todo=todo):
                for stage, half, across in todo:
                    stage(half, 0, across)

        return carry

    lax.fori_loop(0, 16, step_body, 0)

    acc_away = pltpu.make_async_remote_copy(
        src_ref=acc.at[other], dst_ref=accin, send_sem=misc.at[0], recv_sem=misc.at[1], device_id=partner, device_id_type=MESH
    )
    acc_away.start()

    for half in (0, 1):
        stage_own(half, 0, 2)
        stage_far(half, 1, 0)
    for half in (0, 1):
        stage_own(half, 0, 0)

    acc_away.wait_recv()
    cut(
        lambda first, count: (acc[core, first : first + count, :] + accin[first : first + count, :]).astype(BF16),
        hb4,
    )
    round_start(hb4, hb5, rounds[2])
    for half in (0, 1):
        stage_near(half, 1, 0)

    def z_first(zl):
        return pltpu.make_async_remote_copy(
            src_ref=gbuf.at[OWN_SLOT, pl.ds(zl * QUARTER, QUARTER)],
            dst_ref=parts.at[place],
            send_sem=z_send.at[zl],
            recv_sem=z_recv.at[place],
            device_id=me.device(zh=core, zl=zl),
            device_id_type=MESH,
        )

    def not_mine(zl):
        return jnp.logical_not(jnp.logical_and(is_source, me.zl == zl))

    for half in (0, 1):
        stage_own(half, 1, 0)
        for zl in (2 * half, 2 * half + 1):

            @pl.when(not_mine(zl))
            def _(zl=zl):
                z_first(zl).start()

    round_wait(hb4, hb5, rounds[2])
    for s in range(64):
        moved = hb5[moves_ref[1, s]]
        hb6[s] = jnp.where(moves_ref[2, s] > 0, moved, jnp.zeros_like(moved))
    round_start(hb6, hb7, rounds[3])

    def z_second(zl):
        return pltpu.make_async_remote_copy(
            src_ref=pieces.at[me.zl],
            dst_ref=pieces.at[me.zl],
            send_sem=z_send.at[4 + zl],
            recv_sem=z_recv.at[8 + me.zl],
            device_id=me.device(zl=zl),
            device_id_type=MESH,
        )

    def z_third(zl):
        return pltpu.make_async_remote_copy(
            src_ref=pieces.at[zl],
            dst_ref=pieces.at[zl],
            send_sem=z_send.at[8 + zl],
            recv_sem=z_recv.at[12 + zl],
            device_id=partner,
            device_id_type=MESH,
        )

    @pl.when(is_source)
    def _():
        for source in range(8):

            @pl.when(place != source)
            def _(source=source):
                pltpu.make_async_remote_copy(
                    src_ref=parts.at[source],
                    dst_ref=parts.at[source],
                    send_sem=z_send.at[0],
                    recv_sem=z_recv.at[source],
                    device_id=partner,
                    device_id_type=MESH,
                ).wait_recv()

        parts[place] = gbuf[OWN_SLOT, pl.ds(pl.multiple_of(me.zl * QUARTER, QUARTER), QUARTER), :]

        def total_rows(i, carry):
            span = pl.ds(pl.multiple_of(i * 16, 16), 16)
            total = parts[0, span, :].astype(F32)
            for source in range(1, 8):
                total = total + parts[source, span, :].astype(F32)
            pieces[me.zl, span, :] = total.astype(BF16)
            return carry

        lax.fori_loop(0, QUARTER // 16, total_rows, 0)
        for zl in range(4):

            @pl.when(me.zl != zl)
            def _(zl=zl):
                z_second(zl).start()

        for away in range(4):
            zl = (me.zl + away) % 4
            if away:
                pltpu.make_async_remote_copy(
                    src_ref=pieces.at[zl],
                    dst_ref=pieces.at[zl],
                    send_sem=z_send.at[4],
                    recv_sem=z_recv.at[8 + zl],
                    device_id=partner,
                    device_id_type=MESH,
                ).wait_recv()
            z_third(zl).start()

    round_wait(hb6, hb7, rounds[3])
    for t in range(2):
        for i in range(4):
            first = t * STRETCH + 16 * i
            span = slice(OWN + first, OWN + first + 16)
            total = acc[core, span, :] + accin[span, :] + join(hb7, t, i).astype(F32)
            glat_ref[first : first + 16, :] = total.astype(BF16)

    @pl.when(jnp.logical_not(is_source))
    def _():
        for zl in range(4):
            z_third(zl).wait_recv()

    for zl in range(4):
        weight_ref[zl * QUARTER : (zl + 1) * QUARTER, :] = pieces[zl].astype(F32)

    def finish(s, carry):
        away_q(s).wait_send()
        away_go(s).wait_send()
        local_gq(s).wait()
        away_gq(s).wait_send()
        from_gq(s).wait_recv()
        return carry

    lax.fori_loop(0, 16, finish, 0)
    acc_away.wait_send()
    lat_copy(core, OWN).wait_send()
    lat_copy(core, 0).wait_send()
    klo_copy(core).wait_send()
    for i in range(4):
        round_end(hbuf[2 * i], hbuf[2 * i + 1], rounds[i])
    for zl in range(4):

        @pl.when(not_mine(zl))
        def _(zl=zl):
            z_first(zl).wait_send()

        @pl.when(jnp.logical_and(is_source, me.zl != zl))
        def _(zl=zl):
            z_second(zl).wait_send()

        @pl.when(is_source)
        def _(zl=zl):
            z_third(zl).wait_send()

    for args in gather_sends():
        gather_copy(*args).wait_send()
    for plan in plans.values():
        for name in ("0", "1", "back", "ahead"):
            plan[name].wait_send()

    @pl.when(sends_up)
    def _():
        for half in (0, 1):
            for zl in (0, 1):
                z_copy(zl, half).wait_send()

    @pl.when(sends_down)
    def _():
        for half in (0, 1):
            for zl in (3, 2):
                z_copy(zl, half).wait_send()


def main_call(queries, grad_out, latent, klo, moves, weight):
    dma = pltpu.SemaphoreType.DMA
    any_spec = pl.BlockSpec(memory_space=pl.ANY)
    vmem = pl.BlockSpec(memory_space=pltpu.VMEM)
    smem = pl.BlockSpec(memory_space=pltpu.SMEM)
    return pl.pallas_call(
        main_kernel,
        out_shape=(
            jax.ShapeDtypeStruct(queries.shape, BF16),
            jax.ShapeDtypeStruct(latent.shape, BF16),
            jax.ShapeDtypeStruct(weight.shape, F32),
        ),
        in_specs=[any_spec, any_spec, vmem, vmem, smem, vmem],
        out_specs=(any_spec, vmem, vmem),
        scratch_shapes=[
            pltpu.VMEM((16, 2, OWN, QW), BF16),
            pltpu.VMEM((16, 2, OWN, VW), BF16),
            pltpu.VMEM((16, 2, OWN, QW), BF16),
            pltpu.VMEM((2, KEYS, D_ALL), BF16),
            pltpu.VMEM((D_LAT, 2 * KEYS), BF16),
            pltpu.VMEM((2, 8, OWN), F32),
            pltpu.VMEM((2, KEYS, OWN), F32),
            pltpu.VMEM((16, D_LAT, KVW), BF16),
            pltpu.VMEM((16, D_LAT, KVW), BF16),
            pltpu.VMEM((REDUCE_ROWS, KVW), BF16),
            pltpu.VMEM((2 * KEYS, KVW), BF16),
            pltpu.VMEM((2 * KEYS, KVW), BF16),
            pltpu.VMEM((2, KEYS, D_ALL), F32),
            pltpu.VMEM((KEYS, D_ALL), F32),
            *[pltpu.VMEM((64, 16, CUT), BF16)] * 8,
            pltpu.VMEM((8, QUARTER, KVW), BF16),
            pltpu.VMEM((4, QUARTER, KVW), BF16),
        ]
        + [dma((16,))] * 6
        + [dma((6,)), dma((4,)), dma((8, 32)), dma((12,)), dma((16,)), dma((6,))]
        + [dma((len(GATHER),))] * 2
        + [dma((len(REDUCE),))] * 2
        + [dma((16,))] * 3,
        compiler_params=pltpu.CompilerParams(collective_id=0, has_side_effects=True, vmem_limit_bytes=VMEM_LIMIT),
        cost_estimate=pl.CostEstimate(flops=16_000_000_000, bytes_accessed=12_000_000, transcendentals=2_000_000),
        name="attend",
    )(queries, grad_out, latent, klo, moves, weight)


def per_device(queries, grad_out, latent, up_weight, doc_lengths, stretch_order):
    order = stretch_order[0]
    slots = jnp.arange(order.shape[0], dtype=jnp.int32)
    before = jnp.sum(jnp.where(order[None, :] == order[:, None] - 1, slots[None, :], 0), 1)
    after = jnp.sum(jnp.where(order[None, :] == order[:, None] + 1, slots[None, :], 0), 1)
    has_after = order < order.shape[0] - 1

    ends = jnp.cumsum(doc_lengths[0])
    starts = ends - doc_lengths[0]
    me = lax.axis_index("ctx")
    mine = lax.dynamic_slice_in_dim(order, 2 * me, 2)
    position = (mine[:, None] * STRETCH + jnp.arange(STRETCH, dtype=jnp.int32)[None, :]).reshape(OWN)
    start = jnp.max(jnp.where(starts[:, None] <= position[None, :], starts[:, None], 0), 0)
    klo = (start - jnp.repeat(mine, STRETCH) * STRETCH + STRETCH).astype(F32)
    klo = jnp.broadcast_to(klo[None, :], (8, OWN))

    moves = jnp.stack([before, after, has_after.astype(jnp.int32)])
    gq, latent_grad, weight_grad = main_call(queries[0], grad_out[0], latent[0], klo, moves, up_weight)
    return gq[None], latent_grad[None], weight_grad


def solution(mesh):
    in_specs = (
        P("dp", "ctx", None),
        P("dp", "ctx", None),
        P("dp", "ctx", None),
        P(None, "ctx"),
        P("dp", None),
        P("dp", None),
    )
    out_specs = (P("dp", "ctx", None), P("dp", "ctx", None), P(None, "ctx"))
    return jax.shard_map(per_device, mesh=mesh, in_specs=in_specs, out_specs=out_specs, check_vma=False)
```

time: 253 us -> 189 us (0.75)
  waiting for transfers between devices: 30.1 us -> 0 us
  starting transfers between devices: 27.6 us -> 0 us
  local copies, waits for them, and re-layouts: 14.9 us -> 9.9 us
    pallas_call x1, Pallas kernels: 131 us -> 173 us  [main_call(): pl.pallas_call(main_kernel, out_shape=(jax.ShapeDtypeStruct(queries.shape...]
    pallas_call x1 -> x0, Pallas kernels: 41 us -> none  [z_call(): pl.pallas_call(z_kernel, out_shape=jax.ShapeDtypeStruct((D_LAT, KVW), F32...]
    all_to_all x4 -> x0, waiting for transfers between devices: 30.1 us -> none  [the longest x2 18.7 us: spread(): lax.all_to_all(parts, 'ctx', split_axis=0, concat_axis=0, tiled=True)]
    all_to_all x4 -> x0, starting transfers between devices: 27.6 us -> none  [the longest x2 19.3 us: spread(): lax.all_to_all(parts, 'ctx', split_axis=0, concat_axis=0, tiled=True)]
    unnamed x10 -> x6, local copies, waits for them, and re-layouts: 4.79 us -> 8.3 us
    convert_element_type x2 -> x0, local copies, waits for them, and re-layouts: 2.53 us -> none  [per_device(): latent_grad = (glat[OWN:] + returned.astype(F32)).astype(BF16)]
  transfers between devices with their start and end apart: 4 -> 0, of which waited for: 3 -> 0; matrix products, arithmetic and copies ran while one was open for 2% -> 0% of each run, Pallas kernels for 16% -> 0%
where the time goes in v2:
time: 189 us
  Pallas kernels  173 us (92%)
  local copies, waits for them, and re-layouts  9.9 us (5%)
  other arithmetic  4.6 us (2%)
    pallas_call x1, Pallas kernels, main_call(): pl.pallas_call(main_kernel, out_shape=(jax.ShapeDtypeStruct(queries.shape...  173 us
    unnamed x6, local copies, waits for them, and re-layouts  8.3 us

profile of v2, /device:TPU:1, one launch (start us, length us, event | category | flops | bytes accessed | tf_op | source)
XLA Modules:
  0.0 188.5 jit_solution(1808888070053208522)
XLA Ops:
  0.6 0.7 multiply_bitcast_fusion
  1.4 0.7 compare_convert_fusion
  2.0 0.1 iota_add_fusion
  2.1 0.1 add.48
  2.2 0.1 add.45
  2.2 0.1 mul.23
  2.3 0.7 broadcast_add_fusion
  3.0 0.8 select_reduce_fusion.2
  3.8 0.6 pad_add_fusion.moves_ref
  4.4 0.8 copy.16
  5.2 0.2 reduce-window.8
  5.4 0.1 reduce
  5.5 0.7 bitcast_subtract_fusion
  6.1 0.1 select_reduce_fusion
  6.3 0.6 broadcast_in_dim.48.klo_ref
  6.9 1.7 copy.15
  8.6 173.4 %attend.1 = (bf16[128,12288]{1,0:T(8,128)(2,1)}, bf16[128,576]{1,0:T(8,128)(2,1)}, f32[512,512]{1,0:T(8,128)}) custom-call(bf16[128,12288]{1,0:T(8,128)(2,1)} %bitcast.22, bf16[128,8192]{1,0:T(8,128)(2,1)} %bitcast.23, bf16[128,576]{1,0:T(8,128)(2,1)} %bitcast.17, f32[8,128]{1,0:T(8,128)} %broadcast_in_dim.48.klo_ref, s32[3,64]{1,0:T(4,128)} %pad_add_fusion.moves_ref, ...), custom_call_target="tpu_custom_call" | custom-call | flops 16000000000 | bytes 12000000 | tf_op jit(solution)/shard_map/attend/pallas_call | solution.py:838
  181.9 1.7 copy.17
  183.6 0.0 copy-start
  183.6 3.9 %copy.20 = bf16[1,128,12288]{2,1,0:T(8,128)(2,1)} copy(bf16[1,128,12288]{2,1,0:T(8,128)(2,1)} %bitcast.15) | data formatting | bytes 6291456
  187.5 0.0 copy-done
  187.6 1.0 copy.21
  (1 shorter events, 0.0 us)
Async XLA Ops:
  183.6 3.9 %copy-start = (f32[512,512]{1,0:T(8,128)S(1)}, f32[512,512]{1,0:T(8,128)}, u32[]{:S(2)}) copy-start(f32[512,512]{1,0:T(8,128)} %get-tuple-element.27) | copy-start | bytes 3145732

commit v3 on v2

--- a/solution.py
+++ b/solution.py
@@ -29,8 +29,8 @@
 
 
 ORDER = [
-    (1, 0), (0, 1), (1, 1), (1, 3), (3, 1), (2, 1), (1, 2), (2, 0),
-    (0, 2), (2, 3), (3, 2), (2, 2), (3, 3), (3, 0), (0, 3), (0, 0),
+    (1, 0), (0, 1), (1, 1), (1, 3), (3, 1), (2, 1), (1, 2), (2, 3),
+    (3, 2), (2, 2), (2, 0), (0, 2), (3, 3), (3, 0), (0, 3), (0, 0),
 ]
 OWN_SLOT = ORDER.index((0, 0))
 
@@ -119,7 +119,8 @@
     q_hbm,
     go_hbm,
     lat_ref,
-    klo_ref,
+    lens_ref,
+    order_ref,
     moves_ref,
     w_ref,
     gq_hbm,
@@ -173,8 +174,9 @@
     core, other = me.core, 1 - me.core
     partner = me.device(core=other)
     is_source = me.zh == core
-    sends_up = jnp.logical_and(is_source, me.zl == 3)
-    sends_down = jnp.logical_and(is_source, me.zl == 0)
+    at_end = jnp.logical_or(me.zl == 0, me.zl == 3)
+    z_sends = jnp.logical_and(is_source, at_end)
+    z_forwards = jnp.logical_and(jnp.logical_not(is_source), at_end)
     place = me.zh * 4 + me.zl
 
     def ctx_device(away):
@@ -195,27 +197,26 @@
     pl.semaphore_signal(barrier, inc=1, device_id=partner, device_id_type=MESH)
     pl.semaphore_wait(barrier, 38)
 
-    def z_copy(zl, half):
-        return pltpu.make_async_remote_copy(
-            src_ref=w_ref.at[pl.ds(half * HALF, HALF)],
+    def z_copy(source, zh, zl, half):
+        return pltpu.make_async_remote_copy(
+            src_ref=source.at[pl.ds(half * HALF, HALF)],
             dst_ref=wbuf.at[OWN_SLOT, pl.ds(half * HALF, HALF)],
-            send_sem=wz.at[half + 2 * (0 if zl in (0, 3) else 1)],
-            recv_sem=wz.at[4 + half],
-            device_id=me.device(zh=1 - me.zh, zl=zl),
-            device_id_type=MESH,
-        )
-
-    @pl.when(sends_up)
+            send_sem=wz.at[half],
+            recv_sem=wz.at[2 + half],
+            device_id=me.device(zh=zh, zl=zl),
+            device_id_type=MESH,
+        )
+
+    def z_send_copy(half):
+        return z_copy(w_ref, 1 - me.zh, jnp.where(me.zl == 3, 0, 3), half)
+
+    def z_forward(half):
+        return z_copy(wbuf.at[OWN_SLOT], me.zh, jnp.where(me.zl == 0, 1, 2), half)
+
+    @pl.when(z_sends)
     def _():
         for half in (0, 1):
-            for zl in (0, 1):
-                z_copy(zl, half).start()
-
-    @pl.when(sends_down)
-    def _():
-        for half in (0, 1):
-            for zl in (3, 2):
-                z_copy(zl, half).start()
+            z_send_copy(half).start()
 
     def lat_copy(trace, first):
         index = 2 if first else 0
@@ -230,10 +231,10 @@
 
     def klo_copy(trace):
         return pltpu.make_async_remote_copy(
-            src_ref=klo_ref,
+            src_ref=klob.at[trace],
             dst_ref=klob.at[trace],
-            send_sem=misc.at[4],
-            recv_sem=misc.at[5],
+            send_sem=misc.at[2],
+            recv_sem=misc.at[3],
             device_id=partner,
             device_id_type=MESH,
         )
@@ -360,19 +361,20 @@
                 done += [(half, dx, dy, "1", second_axis, -1)]
         return done
 
+    nearest = [(0, 1, 0), (0, 3, 0), (1, 1, 0), (1, 3, 0)]
     events = {
-        0: [(0, 1, 0), (0, 3, 0), (1, 1, 0), (1, 3, 0), (1, 0, 1)],
+        0: [(1, 0, 1)],
         1: [(0, 0, 1), (1, 0, 3), (0, 0, 3)],
         2: [(0, 2, 0), (1, 2, 0), (0, 1, 1), (1, 1, 1)],
         3: [(0, 1, 3), (1, 3, 1)],
         4: [(0, 3, 1), (1, 1, 3)],
         5: [(0, 2, 1), (1, 1, 2), (0, 3, 3), (1, 3, 3)],
-        6: [(0, 1, 2), (1, 2, 1)],
-        7: [(1, 0, 2), (0, 2, 3), (1, 2, 3)],
-        8: [(0, 0, 2)],
-        9: [(1, 3, 2)],
-        10: [(0, 3, 2)],
-        11: [(0, 2, 2), (1, 2, 2)],
+        6: [(0, 1, 2), (1, 2, 1), (0, 2, 3), (1, 2, 3)],
+        7: [(1, 3, 2)],
+        8: [(0, 3, 2)],
+        9: [(0, 2, 2), (1, 2, 2)],
+        10: [(1, 0, 2)],
+        11: [(0, 0, 2)],
     }
 
     def round_copy(source, dest, sems, away):
@@ -422,32 +424,24 @@
             for t in range(2):
                 rows = read(t * STRETCH + 16 * i, 16)
                 for j in range(8):
-                    dest[2 * (8 * i + j) + t] = rows[:, CUT * j : CUT * (j + 1)]
+                    dest[2 * (8 * i + j) + t, :, :CUT] = rows[:, CUT * j : CUT * (j + 1)]
 
     def join(source, t, i):
-        return jnp.concatenate([source[2 * (8 * i + j) + t] for j in range(8)], 1)
+        return jnp.concatenate([source[2 * (8 * i + j) + t, :, :CUT] for j in range(8)], 1)
 
     hbuf = (hb0, hb1, hb2, hb3, hb4, hb5, hb6, hb7)
     rounds = [(hsem.at[2 * i], hsem.at[2 * i + 1]) for i in range(4)]
-    cut(lambda first, count: lat_ref[first : first + count, :], hb0)
-    round_start(hb0, hb1, rounds[0])
-
-    latb[core, OWN:, :] = lat_ref[...]
-    lat_copy(core, OWN).start()
-    klob[core] = klo_ref[...]
-    klo_copy(core).start()
 
     @pl.when(is_source)
     def _():
         wbuf[OWN_SLOT] = w_ref[...]
-
-    @pl.when(jnp.logical_not(is_source))
-    def _():
-        for half in (0, 1):
-            z_copy(0, half).wait_recv()
-
-    gather_event(0, 0, 0)
-    gather_event(1, 0, 0)
+        gather_event(0, 0, 0)
+        gather_event(1, 0, 0)
+
+    latb[core, OWN:, :] = lat_ref[...].T
+    cut(lambda first, count: latb[core, OWN + first : OWN + first + count, :], hb0)
+    round_start(hb0, hb1, rounds[0])
+    lat_copy(core, OWN).start()
 
     def start_tokens(s, carry):
         away_q(s).start()
@@ -458,10 +452,38 @@
 
     lax.fori_loop(0, 16, start_tokens, 0)
 
+    lengths = jnp.broadcast_to(lens_ref[...].astype(F32), (OWN, OWN)).T.astype(BF16)
+    down = lax.broadcasted_iota(jnp.int32, (OWN, OWN), 0)
+    over = lax.broadcasted_iota(jnp.int32, (OWN, OWN), 1)
+    earlier = jnp.where(over < down, 1.0, 0.0).astype(BF16)
+    starts = jnp.dot(earlier, lengths, preferred_element_type=F32)
+    lane = lax.broadcasted_iota(jnp.int32, (1, OWN), 1)
+    first_row = STRETCH * jnp.where(lane < STRETCH, order_ref[0, 2 * me.ctx], order_ref[0, 2 * me.ctx + 1])
+    position = (first_row + lane % STRETCH).astype(F32)
+    begin = jnp.max(jnp.where(starts <= position, starts, 0.0), 0, keepdims=True)
+    klob[core] = jnp.broadcast_to(begin - (first_row - STRETCH).astype(F32), (8, OWN))
+    klo_copy(core).start()
+
     round_wait(hb0, hb1, rounds[0])
     for s in range(64):
-        hb2[s] = hb1[moves_ref[0, s]]
+        hb2[s] = hb1[jnp.maximum(moves_ref[0, s], 0)]
     round_start(hb2, hb3, rounds[1])
+
+    @pl.when(is_source)
+    def _():
+        for event in nearest:
+            gather_event(*event)
+
+    @pl.when(jnp.logical_not(is_source))
+    def _():
+        for half in (0, 1):
+            z_copy(w_ref, me.zh, me.zl, half).wait_recv()
+
+            @pl.when(at_end)
+            def _(half=half):
+                z_forward(half).start()
+
+            gather_event(half, 0, 0)
 
     klo_copy(other).wait_recv()
     key = lax.broadcasted_iota(jnp.int32, (KEYS, OWN), 0)
@@ -584,16 +606,23 @@
         add_rows(own, first, count, sources)
 
     sums = {
-        5: [(stage_far, 1, 1)],
-        6: [(stage_far, 0, 1)],
-        7: [(stage_far, 1, 0), (stage_near, 1, 1)],
-        8: [(stage_far, 0, 0), (stage_near, 0, 1)],
-        9: [(stage_far, 1, 3), (stage_own, 1, 1)],
-        10: [(stage_far, 0, 3), (stage_own, 0, 1)],
-        11: [(stage_far, 0, 2), (stage_far, 1, 2)],
-        12: [(stage_near, 1, 3), (stage_near, 0, 3)],
-        13: [(stage_near, 0, 2), (stage_near, 1, 2), (stage_near, 1, 0)],
-        14: [(stage_near, 0, 0), (stage_own, 0, 3), (stage_own, 1, 3)],
+        5: [(stage_far, 1, 0, 1)],
+        6: [(stage_far, 0, 0, 1)],
+        7: [(stage_far, 1, 0, 3), (stage_near, 1, 0, 1)],
+        8: [(stage_far, 0, 0, 3), (stage_near, 0, 0, 1)],
+        9: [(stage_far, 0, 0, 2), (stage_far, 1, 0, 2), (stage_own, 1, 0, 1)],
+        10: [(stage_far, 1, 0, 0), (stage_own, 0, 0, 1)],
+        11: [(stage_far, 0, 0, 0), (stage_near, 0, 0, 2), (stage_near, 1, 0, 2)],
+        12: [(stage_near, 0, 0, 3), (stage_near, 1, 0, 3)],
+        13: [
+            (stage_own, 0, 0, 2),
+            (stage_far, 0, 1, 0),
+            (stage_own, 1, 0, 2),
+            (stage_far, 1, 1, 0),
+            (stage_near, 1, 0, 0),
+        ],
+        14: [(stage_near, 0, 0, 0), (stage_own, 0, 0, 3), (stage_own, 1, 0, 3)],
+        15: [(stage_near, 0, 1, 0), (stage_near, 1, 1, 0)],
     }
 
     def step_body(s, carry):
@@ -601,7 +630,14 @@
             if todo:
 
                 @pl.when(s == at_step)
-                def _(todo=todo):
+                def _(todo=todo, at_step=at_step):
+                    if at_step == 0:
+
+                        @pl.when(jnp.logical_not(is_source))
+                        def _():
+                            for event in nearest:
+                                gather_event(*event)
+
                     for event in todo:
                         gather_event(*event)
 
@@ -647,8 +683,8 @@
 
             @pl.when(s == at_step)
             def _(todo=todo):
-                for stage, half, across in todo:
-                    stage(half, 0, across)
+                for stage, half, phase, across in todo:
+                    stage(half, phase, across)
 
         return carry
 
@@ -659,11 +695,27 @@
     )
     acc_away.start()
 
-    for half in (0, 1):
-        stage_own(half, 0, 2)
-        stage_far(half, 1, 0)
+    def z_first(zl):
+        return pltpu.make_async_remote_copy(
+            src_ref=gbuf.at[OWN_SLOT, pl.ds(zl * QUARTER, QUARTER)],
+            dst_ref=parts.at[place],
+            send_sem=z_send.at[zl],
+            recv_sem=z_recv.at[place],
+            device_id=me.device(zh=core, zl=zl),
+            device_id_type=MESH,
+        )
+
+    def not_mine(zl):
+        return jnp.logical_not(jnp.logical_and(is_source, me.zl == zl))
+
     for half in (0, 1):
         stage_own(half, 0, 0)
+        stage_own(half, 1, 0)
+        for zl in (2 * half, 2 * half + 1):
+
+            @pl.when(not_mine(zl))
+            def _(zl=zl):
+                z_first(zl).start()
 
     acc_away.wait_recv()
     cut(
@@ -671,34 +723,11 @@
         hb4,
     )
     round_start(hb4, hb5, rounds[2])
-    for half in (0, 1):
-        stage_near(half, 1, 0)
-
-    def z_first(zl):
-        return pltpu.make_async_remote_copy(
-            src_ref=gbuf.at[OWN_SLOT, pl.ds(zl * QUARTER, QUARTER)],
-            dst_ref=parts.at[place],
-            send_sem=z_send.at[zl],
-            recv_sem=z_recv.at[place],
-            device_id=me.device(zh=core, zl=zl),
-            device_id_type=MESH,
-        )
-
-    def not_mine(zl):
-        return jnp.logical_not(jnp.logical_and(is_source, me.zl == zl))
-
-    for half in (0, 1):
-        stage_own(half, 1, 0)
-        for zl in (2 * half, 2 * half + 1):
-
-            @pl.when(not_mine(zl))
-            def _(zl=zl):
-                z_first(zl).start()
 
     round_wait(hb4, hb5, rounds[2])
     for s in range(64):
-        moved = hb5[moves_ref[1, s]]
-        hb6[s] = jnp.where(moves_ref[2, s] > 0, moved, jnp.zeros_like(moved))
+        moved = hb5[jnp.maximum(moves_ref[1, s], 0)]
+        hb6[s] = jnp.where(moves_ref[1, s] >= 0, moved, jnp.zeros_like(moved))
     round_start(hb6, hb7, rounds[3])
 
     def z_second(zl):
@@ -771,8 +800,8 @@
         for i in range(4):
             first = t * STRETCH + 16 * i
             span = slice(OWN + first, OWN + first + 16)
-            total = acc[core, span, :] + accin[span, :] + join(hb7, t, i).astype(F32)
-            glat_ref[first : first + 16, :] = total.astype(BF16)
+            accin[span, :] += acc[core, span, :] + join(hb7, t, i).astype(F32)
+    glat_ref[...] = accin[OWN:, :].T.astype(BF16)
 
     @pl.when(jnp.logical_not(is_source))
     def _():
@@ -817,20 +846,18 @@
         for name in ("0", "1", "back", "ahead"):
             plan[name].wait_send()
 
-    @pl.when(sends_up)
+    @pl.when(z_sends)
     def _():
         for half in (0, 1):
-            for zl in (0, 1):
-                z_copy(zl, half).wait_send()
-
-    @pl.when(sends_down)
+            z_send_copy(half).wait_send()
+
+    @pl.when(z_forwards)
     def _():
         for half in (0, 1):
-            for zl in (3, 2):
-                z_copy(zl, half).wait_send()
-
-
-def main_call(queries, grad_out, latent, klo, moves, weight):
+            z_forward(half).wait_send()
+
+
+def main_call(queries, grad_out, latent, lengths, order, moves, weight):
     dma = pltpu.SemaphoreType.DMA
     any_spec = pl.BlockSpec(memory_space=pl.ANY)
     vmem = pl.BlockSpec(memory_space=pltpu.VMEM)
@@ -842,7 +869,7 @@
             jax.ShapeDtypeStruct(latent.shape, BF16),
             jax.ShapeDtypeStruct(weight.shape, F32),
         ),
-        in_specs=[any_spec, any_spec, vmem, vmem, smem, vmem],
+        in_specs=[any_spec, any_spec, vmem, vmem, smem, smem, vmem],
         out_specs=(any_spec, vmem, vmem),
         scratch_shapes=[
             pltpu.VMEM((16, 2, OWN, QW), BF16),
@@ -859,40 +886,30 @@
             pltpu.VMEM((2 * KEYS, KVW), BF16),
             pltpu.VMEM((2, KEYS, D_ALL), F32),
             pltpu.VMEM((KEYS, D_ALL), F32),
-            *[pltpu.VMEM((64, 16, CUT), BF16)] * 8,
+            *[pltpu.VMEM((64, 16, 128), BF16)] * 8,
             pltpu.VMEM((8, QUARTER, KVW), BF16),
             pltpu.VMEM((4, QUARTER, KVW), BF16),
         ]
         + [dma((16,))] * 6
-        + [dma((6,)), dma((4,)), dma((8, 32)), dma((12,)), dma((16,)), dma((6,))]
+        + [dma((4,)), dma((4,)), dma((8, 32)), dma((12,)), dma((16,)), dma((4,))]
         + [dma((len(GATHER),))] * 2
         + [dma((len(REDUCE),))] * 2
         + [dma((16,))] * 3,
         compiler_params=pltpu.CompilerParams(collective_id=0, has_side_effects=True, vmem_limit_bytes=VMEM_LIMIT),
         cost_estimate=pl.CostEstimate(flops=16_000_000_000, bytes_accessed=12_000_000, transcendentals=2_000_000),
         name="attend",
-    )(queries, grad_out, latent, klo, moves, weight)
+    )(queries, grad_out, latent, lengths, order, moves, weight)
 
 
 def per_device(queries, grad_out, latent, up_weight, doc_lengths, stretch_order):
     order = stretch_order[0]
     slots = jnp.arange(order.shape[0], dtype=jnp.int32)
-    before = jnp.sum(jnp.where(order[None, :] == order[:, None] - 1, slots[None, :], 0), 1)
-    after = jnp.sum(jnp.where(order[None, :] == order[:, None] + 1, slots[None, :], 0), 1)
-    has_after = order < order.shape[0] - 1
-
-    ends = jnp.cumsum(doc_lengths[0])
-    starts = ends - doc_lengths[0]
-    me = lax.axis_index("ctx")
-    mine = lax.dynamic_slice_in_dim(order, 2 * me, 2)
-    position = (mine[:, None] * STRETCH + jnp.arange(STRETCH, dtype=jnp.int32)[None, :]).reshape(OWN)
-    start = jnp.max(jnp.where(starts[:, None] <= position[None, :], starts[:, None], 0), 0)
-    klo = (start - jnp.repeat(mine, STRETCH) * STRETCH + STRETCH).astype(F32)
-    klo = jnp.broadcast_to(klo[None, :], (8, OWN))
-
-    moves = jnp.stack([before, after, has_after.astype(jnp.int32)])
-    gq, latent_grad, weight_grad = main_call(queries[0], grad_out[0], latent[0], klo, moves, up_weight)
-    return gq[None], latent_grad[None], weight_grad
+    wanted = order[None, :] + jnp.array([[-1], [1]], jnp.int32)
+    moves = jnp.sum(jnp.where(order[None, None, :] == wanted[:, :, None], slots[None, None, :] + 1, 0), 2) - 1
+    gq, latent_grad, weight_grad = main_call(
+        queries[0], grad_out[0], latent[0].T, doc_lengths, stretch_order, moves, up_weight
+    )
+    return gq[None], latent_grad.T[None], weight_grad
 
 
 def solution(mesh):

time: 189 us -> 164 us (0.87)
  Pallas kernels: 173 us -> 155 us
  local copies, waits for them, and re-layouts: 9.9 us -> 5.57 us
  other arithmetic: 4.6 us -> 2.16 us
    pallas_call x1, Pallas kernels: 173 us -> 155 us  [main_call(): pl.pallas_call(main_kernel, out_shape=(jax.ShapeDtypeStruct(queries.shape...]
    unnamed x6 -> x7, local copies, waits for them, and re-layouts: 8.3 us -> 5.57 us
where the time goes in v3:
time: 164 us
  Pallas kernels  155 us (95%)
  local copies, waits for them, and re-layouts  5.57 us (3%)
  other arithmetic  2.16 us (1%)
    pallas_call x1, Pallas kernels, main_call(): pl.pallas_call(main_kernel, out_shape=(jax.ShapeDtypeStruct(queries.shape...  155 us
    unnamed x7, local copies, waits for them, and re-layouts  5.57 us

profile of v3, /device:TPU:1, one launch (start us, length us, event | category | flops | bytes accessed | tf_op | source)
XLA Modules:
  0.0 163.8 jit_solution(4637214541222607056)
XLA Ops:
  0.6 0.7 broadcast_add_fusion.1
  1.4 0.8 select_reduce_fusion
  2.2 0.6 broadcast_add_fusion.moves_ref
  2.8 155.4 %attend.1 = (bf16[128,12288]{1,0:T(8,128)(2,1)}, bf16[576,128]{1,0:T(8,128)(2,1)}, f32[512,512]{1,0:T(8,128)}) custom-call(bf16[128,12288]{1,0:T(8,128)(2,1)} %bitcast.14, bf16[128,8192]{1,0:T(8,128)(2,1)} %bitcast.15, bf16[576,128]{1,0:T(8,128)(2,1)} %bitcast.16, s32[1,128]{1,0:T(1,128)} %lens_ref.1, s32[1,64]{1,0:T(1,128)} %order_ref.1, ...), custom_call_target="tpu_custom_call" | custom-call | flops 16000000000 | bytes 12000000 | tf_op jit(solution)/shard_map/attend/pallas_call | solution.py:865
  158.2 0.0 copy-start.1
  158.2 0.0 copy-start
  158.2 3.9 %copy.13 = bf16[1,128,12288]{2,1,0:T(8,128)(2,1)} copy(bf16[1,128,12288]{2,1,0:T(8,128)(2,1)} %bitcast.10) | data formatting | bytes 6291456
  162.1 0.0 copy-done.1
  162.1 0.7 copy.14
  162.8 0.0 copy-done
  162.8 1.0 copy.15
  (1 shorter events, 0.0 us)
Async XLA Ops:
  158.2 4.0 %copy-start.1 = (bf16[576,128]{1,0:T(8,128)(2,1)S(1)}, bf16[576,128]{1,0:T(8,128)(2,1)}, u32[]{:S(2)}) copy-start(bf16[576,128]{1,0:T(8,128)(2,1)} %get-tuple-element.7) | copy-start | bytes 442372
  158.2 4.6 %copy-start = (f32[512,512]{1,0:T(8,128)S(1)}, f32[512,512]{1,0:T(8,128)}, u32[]{:S(2)}) copy-start(f32[512,512]{1,0:T(8,128)} %get-tuple-element.14) | copy-start | bytes 3145732

commit v4 on v3

--- a/solution.py
+++ b/solution.py
@@ -148,6 +148,8 @@
     hb5,
     hb6,
     hb7,
+    moves_in,
+    moves,
     parts,
     pieces,
     loc_q,
@@ -157,6 +159,7 @@
     snd_q,
     snd_go,
     misc,
+    move_sem,
     lat_sem,
     hsem,
     z_send,
@@ -179,23 +182,72 @@
     z_forwards = jnp.logical_and(jnp.logical_not(is_source), at_end)
     place = me.zh * 4 + me.zl
 
-    def ctx_device(away):
-        return (me.dp, (me.ctx + away) % 32)
+    def mover(ctx):
+        return (((me.zl + 2) % 4) * 2 + core, ctx)
 
     barrier = pltpu.get_barrier_semaphore()
 
     def greet(away, carry):
-        pl.semaphore_signal(barrier, inc=1, device_id=ctx_device(away), device_id_type=MESH)
+        pl.semaphore_signal(barrier, inc=1, device_id=mover((me.ctx + away) % 32), device_id_type=MESH)
         return carry
 
-    lax.fori_loop(1, 32, greet, 0)
-    for away in (1, 2, 3):
+    lax.fori_loop(0, 32, greet, 0)
+    for away in (1, 3):
         for zh in (me.zh, 1 - me.zh):
             pl.semaphore_signal(
                 barrier, inc=1, device_id=me.device(zh=zh, zl=(me.zl + away) % 4), device_id_type=MESH
             )
+    pl.semaphore_signal(barrier, inc=1, device_id=me.device(zh=1 - me.zh), device_id_type=MESH)
+    for axis in ("x", "y"):
+        for sign in (1, -1):
+            pl.semaphore_signal(barrier, inc=1, device_id=me.neighbour(axis, sign), device_id_type=MESH)
     pl.semaphore_signal(barrier, inc=1, device_id=partner, device_id_type=MESH)
-    pl.semaphore_wait(barrier, 38)
+    def group_of(step, half):
+        dx, dy = pick(step, [d[0] for d in ORDER]), pick(step, [d[1] for d in ORDER])
+        return (((me.x + dx) % 4) * 2 + half) * 4 + (me.y + dy) % 4
+
+    def columns(step, half, width):
+        return pl.ds(pl.multiple_of(group_of(step, half) * width, width), width)
+
+    def own_q(s):
+        return pltpu.make_async_copy(q_hbm.at[:, columns(s, core, QW)], qbuf.at[s, core], loc_q.at[s])
+
+    def own_go(s):
+        return pltpu.make_async_copy(go_hbm.at[:, columns(s, core, VW)], gobuf.at[s, core], loc_go.at[s])
+
+    def cut(read, dest):
+        for i in range(4):
+            for t in range(2):
+                rows = read(t * STRETCH + 16 * i, 16)
+                for j in range(8):
+                    dest[2 * (8 * i + j) + t, :, :CUT] = rows[:, CUT * j : CUT * (j + 1)]
+
+    def start_own(s, carry):
+        own_q(s).start()
+        own_go(s).start()
+        return carry
+
+    lax.fori_loop(0, 16, start_own, 0)
+    latb[core, OWN:, :] = lat_ref[...].T
+    cut(lambda first, count: latb[core, OWN + first : OWN + first + count, :], hb0)
+
+    lengths = jnp.broadcast_to(lens_ref[...].astype(F32), (OWN, OWN)).T.astype(BF16)
+    down = lax.broadcasted_iota(jnp.int32, (OWN, OWN), 0)
+    over = lax.broadcasted_iota(jnp.int32, (OWN, OWN), 1)
+    earlier = jnp.where(over < down, 1.0, 0.0).astype(BF16)
+    starts = jnp.dot(earlier, lengths, preferred_element_type=F32)
+    lane = lax.broadcasted_iota(jnp.int32, (1, OWN), 1)
+    first_row = STRETCH * jnp.where(lane < STRETCH, order_ref[0, 2 * me.ctx], order_ref[0, 2 * me.ctx + 1])
+    position = (first_row + lane % STRETCH).astype(F32)
+    begin = jnp.max(jnp.where(starts <= position, starts, 0.0), 0, keepdims=True)
+    klob[core] = jnp.broadcast_to(begin - (first_row - STRETCH).astype(F32), (8, OWN))
+    acc[...] = jnp.zeros_like(acc)
+
+    @pl.when(is_source)
+    def _():
+        wbuf[OWN_SLOT] = w_ref[...]
+
+    pl.semaphore_wait(barrier, 42)
 
     def z_copy(source, zh, zl, half):
         return pltpu.make_async_remote_copy(
@@ -238,19 +290,6 @@
             device_id=partner,
             device_id_type=MESH,
         )
-
-    def group_of(step, half):
-        dx, dy = pick(step, [d[0] for d in ORDER]), pick(step, [d[1] for d in ORDER])
-        return (((me.x + dx) % 4) * 2 + half) * 4 + (me.y + dy) % 4
-
-    def columns(step, half, width):
-        return pl.ds(pl.multiple_of(group_of(step, half) * width, width), width)
-
-    def own_q(s):
-        return pltpu.make_async_copy(q_hbm.at[:, columns(s, core, QW)], qbuf.at[s, core], loc_q.at[s])
-
-    def own_go(s):
-        return pltpu.make_async_copy(go_hbm.at[:, columns(s, core, VW)], gobuf.at[s, core], loc_go.at[s])
 
     def away_q(s):
         return pltpu.make_async_remote_copy(
@@ -362,8 +401,9 @@
         return done
 
     nearest = [(0, 1, 0), (0, 3, 0), (1, 1, 0), (1, 3, 0)]
+    early = {True: nearest + [(1, 0, 1), (0, 0, 1), (1, 0, 3), (0, 0, 3)], False: []}
     events = {
-        0: [(1, 0, 1)],
+        0: nearest + [(1, 0, 1)],
         1: [(0, 0, 1), (1, 0, 3), (0, 0, 3)],
         2: [(0, 2, 0), (1, 2, 0), (0, 1, 1), (1, 1, 1)],
         3: [(0, 1, 3), (1, 3, 1)],
@@ -377,54 +417,53 @@
         11: [(0, 0, 2)],
     }
 
-    def round_copy(source, dest, sems, away):
-        to = (me.ctx + away) % 32
+    def round_copy(source, dest, sems, to):
         return pltpu.make_async_remote_copy(
             src_ref=source.at[pl.ds(2 * to, 2)],
             dst_ref=dest.at[pl.ds(2 * me.ctx, 2)],
-            send_sem=sems[0].at[away],
-            recv_sem=sems[1].at[away],
-            device_id=ctx_device(away),
+            send_sem=sems[0].at[to],
+            recv_sem=sems[1].at[me.ctx],
+            device_id=mover(to),
             device_id_type=MESH,
         )
 
     def round_start(source, dest, sems):
         def go(away, carry):
-            round_copy(source, dest, sems, away).start()
+            round_copy(source, dest, sems, (me.ctx + away) % 32).start()
             return carry
 
-        lax.fori_loop(1, 32, go, 0)
-        for t in range(2):
-            dest[2 * me.ctx + t] = source[2 * me.ctx + t]
+        lax.fori_loop(0, 32, go, 0)
 
     def round_wait(source, dest, sems):
-        def go(away, carry):
-            frm = (me.ctx + 32 - away) % 32
+        def go(frm, carry):
             pltpu.make_async_remote_copy(
                 src_ref=source.at[pl.ds(2 * frm, 2)],
                 dst_ref=dest.at[pl.ds(2 * frm, 2)],
-                send_sem=sems[0].at[away],
-                recv_sem=sems[1].at[away],
-                device_id=ctx_device(away),
+                send_sem=sems[0].at[frm],
+                recv_sem=sems[1].at[frm],
+                device_id=mover(frm),
                 device_id_type=MESH,
             ).wait_recv()
             return carry
 
-        lax.fori_loop(1, 32, go, 0)
+        lax.fori_loop(0, 32, go, 0)
 
     def round_end(source, dest, sems):
-        def go(away, carry):
-            round_copy(source, dest, sems, away).wait_send()
+        def go(to, carry):
+            round_copy(source, dest, sems, to).wait_send()
             return carry
 
-        lax.fori_loop(1, 32, go, 0)
-
-    def cut(read, dest):
-        for i in range(4):
-            for t in range(2):
-                rows = read(t * STRETCH + 16 * i, 16)
-                for j in range(8):
-                    dest[2 * (8 * i + j) + t, :, :CUT] = rows[:, CUT * j : CUT * (j + 1)]
+        lax.fori_loop(0, 32, go, 0)
+
+    moves_away = pltpu.make_async_remote_copy(
+        src_ref=moves_ref,
+        dst_ref=moves_in,
+        send_sem=move_sem.at[0],
+        recv_sem=move_sem.at[1],
+        device_id=mover(me.ctx),
+        device_id_type=MESH,
+    )
+    moves_here = pltpu.make_async_copy(moves_in, moves, move_sem.at[2])
 
     def join(source, t, i):
         return jnp.concatenate([source[2 * (8 * i + j) + t, :, :CUT] for j in range(8)], 1)
@@ -432,46 +471,35 @@
     hbuf = (hb0, hb1, hb2, hb3, hb4, hb5, hb6, hb7)
     rounds = [(hsem.at[2 * i], hsem.at[2 * i + 1]) for i in range(4)]
 
+    moves_away.start()
+    round_start(hb0, hb1, rounds[0])
+
     @pl.when(is_source)
     def _():
-        wbuf[OWN_SLOT] = w_ref[...]
         gather_event(0, 0, 0)
         gather_event(1, 0, 0)
 
-    latb[core, OWN:, :] = lat_ref[...].T
-    cut(lambda first, count: latb[core, OWN + first : OWN + first + count, :], hb0)
-    round_start(hb0, hb1, rounds[0])
     lat_copy(core, OWN).start()
+    klo_copy(core).start()
 
     def start_tokens(s, carry):
         away_q(s).start()
         away_go(s).start()
-        own_q(s).start()
-        own_go(s).start()
         return carry
 
     lax.fori_loop(0, 16, start_tokens, 0)
 
-    lengths = jnp.broadcast_to(lens_ref[...].astype(F32), (OWN, OWN)).T.astype(BF16)
-    down = lax.broadcasted_iota(jnp.int32, (OWN, OWN), 0)
-    over = lax.broadcasted_iota(jnp.int32, (OWN, OWN), 1)
-    earlier = jnp.where(over < down, 1.0, 0.0).astype(BF16)
-    starts = jnp.dot(earlier, lengths, preferred_element_type=F32)
-    lane = lax.broadcasted_iota(jnp.int32, (1, OWN), 1)
-    first_row = STRETCH * jnp.where(lane < STRETCH, order_ref[0, 2 * me.ctx], order_ref[0, 2 * me.ctx + 1])
-    position = (first_row + lane % STRETCH).astype(F32)
-    begin = jnp.max(jnp.where(starts <= position, starts, 0.0), 0, keepdims=True)
-    klob[core] = jnp.broadcast_to(begin - (first_row - STRETCH).astype(F32), (8, OWN))
-    klo_copy(core).start()
-
+    moves_away.wait_recv()
+    moves_here.start()
+    moves_here.wait()
     round_wait(hb0, hb1, rounds[0])
     for s in range(64):
-        hb2[s] = hb1[jnp.maximum(moves_ref[0, s], 0)]
+        hb2[s] = hb1[jnp.maximum(moves[0, s], 0)]
     round_start(hb2, hb3, rounds[1])
 
     @pl.when(is_source)
     def _():
-        for event in nearest:
+        for event in early[True]:
             gather_event(*event)
 
     @pl.when(jnp.logical_not(is_source))
@@ -494,7 +522,6 @@
     for trace in range(2):
         allowed = same & (spot <= latest) & (spot >= klob[trace, 0:1, :])
         bias[trace] = jnp.where(allowed, 0.0, -jnp.inf)
-    acc[...] = jnp.zeros_like(acc)
 
     round_wait(hb2, hb3, rounds[1])
     for t in range(2):
@@ -630,16 +657,17 @@
             if todo:
 
                 @pl.when(s == at_step)
-                def _(todo=todo, at_step=at_step):
-                    if at_step == 0:
-
-                        @pl.when(jnp.logical_not(is_source))
-                        def _():
-                            for event in nearest:
+                def _(todo=todo):
+                    for event in todo:
+                        if event in early[True] and event in early[False]:
+                            continue
+                        if event in early[True]:
+
+                            @pl.when(jnp.logical_not(is_source))
+                            def _(event=event):
                                 gather_event(*event)
-
-                    for event in todo:
-                        gather_event(*event)
+                        else:
+                            gather_event(*event)
 
         own_q(s).wait()
         own_go(s).wait()
@@ -695,28 +723,6 @@
     )
     acc_away.start()
 
-    def z_first(zl):
-        return pltpu.make_async_remote_copy(
-            src_ref=gbuf.at[OWN_SLOT, pl.ds(zl * QUARTER, QUARTER)],
-            dst_ref=parts.at[place],
-            send_sem=z_send.at[zl],
-            recv_sem=z_recv.at[place],
-            device_id=me.device(zh=core, zl=zl),
-            device_id_type=MESH,
-        )
-
-    def not_mine(zl):
-        return jnp.logical_not(jnp.logical_and(is_source, me.zl == zl))
-
-    for half in (0, 1):
-        stage_own(half, 0, 0)
-        stage_own(half, 1, 0)
-        for zl in (2 * half, 2 * half + 1):
-
-            @pl.when(not_mine(zl))
-            def _(zl=zl):
-                z_first(zl).start()
-
     acc_away.wait_recv()
     cut(
         lambda first, count: (acc[core, first : first + count, :] + accin[first : first + count, :]).astype(BF16),
@@ -724,10 +730,32 @@
     )
     round_start(hb4, hb5, rounds[2])
 
+    def z_first(zl):
+        return pltpu.make_async_remote_copy(
+            src_ref=gbuf.at[OWN_SLOT, pl.ds(zl * QUARTER, QUARTER)],
+            dst_ref=parts.at[place],
+            send_sem=z_send.at[zl],
+            recv_sem=z_recv.at[place],
+            device_id=me.device(zh=core, zl=zl),
+            device_id_type=MESH,
+        )
+
+    def not_mine(zl):
+        return jnp.logical_not(jnp.logical_and(is_source, me.zl == zl))
+
+    for half in (0, 1):
+        stage_own(half, 0, 0)
+        stage_own(half, 1, 0)
+        for zl in (2 * half, 2 * half + 1):
+
+            @pl.when(not_mine(zl))
+            def _(zl=zl):
+                z_first(zl).start()
+
     round_wait(hb4, hb5, rounds[2])
     for s in range(64):
-        moved = hb5[jnp.maximum(moves_ref[1, s], 0)]
-        hb6[s] = jnp.where(moves_ref[1, s] >= 0, moved, jnp.zeros_like(moved))
+        moved = hb5[jnp.maximum(moves[1, s], 0)]
+        hb6[s] = jnp.where(moves[1, s] >= 0, moved, jnp.zeros_like(moved))
     round_start(hb6, hb7, rounds[3])
 
     def z_second(zl):
@@ -821,6 +849,7 @@
 
     lax.fori_loop(0, 16, finish, 0)
     acc_away.wait_send()
+    moves_away.wait_send()
     lat_copy(core, OWN).wait_send()
     lat_copy(core, 0).wait_send()
     klo_copy(core).wait_send()
@@ -869,7 +898,7 @@
             jax.ShapeDtypeStruct(latent.shape, BF16),
             jax.ShapeDtypeStruct(weight.shape, F32),
         ),
-        in_specs=[any_spec, any_spec, vmem, vmem, smem, smem, vmem],
+        in_specs=[any_spec, any_spec, vmem, vmem, smem, vmem, vmem],
         out_specs=(any_spec, vmem, vmem),
         scratch_shapes=[
             pltpu.VMEM((16, 2, OWN, QW), BF16),
@@ -887,11 +916,13 @@
             pltpu.VMEM((2, KEYS, D_ALL), F32),
             pltpu.VMEM((KEYS, D_ALL), F32),
             *[pltpu.VMEM((64, 16, 128), BF16)] * 8,
+            pltpu.VMEM((8, 128), jnp.int32),
+            pltpu.SMEM((8, 128), jnp.int32),
             pltpu.VMEM((8, QUARTER, KVW), BF16),
             pltpu.VMEM((4, QUARTER, KVW), BF16),
         ]
         + [dma((16,))] * 6
-        + [dma((4,)), dma((4,)), dma((8, 32)), dma((12,)), dma((16,)), dma((4,))]
+        + [dma((4,)), dma((3,)), dma((4,)), dma((8, 32)), dma((12,)), dma((16,)), dma((4,))]
         + [dma((len(GATHER),))] * 2
         + [dma((len(REDUCE),))] * 2
         + [dma((16,))] * 3,
@@ -906,6 +937,7 @@
     slots = jnp.arange(order.shape[0], dtype=jnp.int32)
     wanted = order[None, :] + jnp.array([[-1], [1]], jnp.int32)
     moves = jnp.sum(jnp.where(order[None, None, :] == wanted[:, :, None], slots[None, None, :] + 1, 0), 2) - 1
+    moves = jnp.pad(moves, ((0, 6), (0, 64)))
     gq, latent_grad, weight_grad = main_call(
         queries[0], grad_out[0], latent[0].T, doc_lengths, stretch_order, moves, up_weight
     )

time: 164 us -> 160 us (0.976)
  Pallas kernels: 155 us -> 151 us
    pallas_call x1, Pallas kernels: 155 us -> 151 us  [main_call(): pl.pallas_call(main_kernel, out_shape=(jax.ShapeDtypeStruct(queries.shape...]
where the time goes in v4:
time: 160 us
  Pallas kernels  151 us (94%)
  local copies, waits for them, and re-layouts  6.17 us (4%)
    pallas_call x1, Pallas kernels, main_call(): pl.pallas_call(main_kernel, out_shape=(jax.ShapeDtypeStruct(queries.shape...  151 us
    unnamed x7, local copies, waits for them, and re-layouts  5.57 us

profile of v4, /device:TPU:1, one launch (start us, length us, event | category | flops | bytes accessed | tf_op | source)
XLA Modules:
  0.0 159.8 jit_solution(11911854461153405270)
XLA Ops:
  0.6 0.7 broadcast_add_fusion.1
  1.4 0.8 select_reduce_fusion
  2.2 0.6 pad.4.moves_ref
  2.8 151.3 %attend.1 = (bf16[128,12288]{1,0:T(8,128)(2,1)}, bf16[576,128]{1,0:T(8,128)(2,1)}, f32[512,512]{1,0:T(8,128)}) custom-call(bf16[128,12288]{1,0:T(8,128)(2,1)} %bitcast.14, bf16[128,8192]{1,0:T(8,128)(2,1)} %bitcast.15, bf16[576,128]{1,0:T(8,128)(2,1)} %bitcast.16, s32[1,128]{1,0:T(1,128)} %lens_ref.1, s32[1,64]{1,0:T(1,128)} %order_ref.1, ...), custom_call_target="tpu_custom_call" | custom-call | flops 16000000000 | bytes 12000000 | tf_op jit(solution)/shard_map/attend/pallas_call | solution.py:894
  154.2 0.0 copy-start.1
  154.2 0.0 copy-start
  154.2 3.9 %copy.13 = bf16[1,128,12288]{2,1,0:T(8,128)(2,1)} copy(bf16[1,128,12288]{2,1,0:T(8,128)(2,1)} %bitcast.10) | data formatting | bytes 6291456
  158.1 0.0 copy-done.1
  158.1 0.7 copy.14
  158.8 0.0 copy-done
  158.8 1.0 copy.15
  (2 shorter events, 0.0 us)
Async XLA Ops:
  154.2 4.0 %copy-start.1 = (bf16[576,128]{1,0:T(8,128)(2,1)S(1)}, bf16[576,128]{1,0:T(8,128)(2,1)}, u32[]{:S(2)}) copy-start(bf16[576,128]{1,0:T(8,128)(2,1)} %get-tuple-element.7) | copy-start | bytes 442372
  154.2 4.6 %copy-start = (f32[512,512]{1,0:T(8,128)S(1)}, f32[512,512]{1,0:T(8,128)}, u32[]{:S(2)}) copy-start(f32[512,512]{1,0:T(8,128)} %get-tuple-element.14) | copy-start | bytes 3145732
